TPU v7x, 32 devices: a whole 2x2x4 slice. The times are simulated.
32 devices in a mesh: dp: 8 (over z, x), tensor: 4 (over y, core).
Axes of the slice: x: 2, y: 2, z: 4, core: 2. Of those that a mesh axis runs over, the one named last changes fastest.
Arguments:
- tokens: bfloat16 [12608, 512], P(('dp', 'tensor')), may hold values from -6 to 6
- cotangent: bfloat16 [12608, 512], P(('dp', 'tensor')), may hold values from -6 to 6
- norm_gain: float32 [2, 512], replicated, may hold values from 0.1 to 1.9
- qkv_weight: bfloat16 [3, 512, 512], P(None, 'dp', 'tensor'), may hold values from -0.25 to 0.25
- out_weight: bfloat16 [512, 512], P('dp', 'tensor'), may hold values from -1 to 1
- expert_in: bfloat16 [8, 512, 2048], P(None, 'dp', 'tensor'), may hold values from -0.25 to 0.25
- expert_out: bfloat16 [8, 512, 2048], P(None, 'dp', 'tensor'), may hold values from -1 to 1
- router_weight: bfloat16 [512, 8], replicated, may hold values from -0.125 to 0.125
- down_in: bfloat16 [5, 8, 512, 16], replicated, may hold values from -0.25 to 0.25
- up_heads: bfloat16 [3, 8, 16, 512], P(None, None, None, 'tensor'), may hold values from -1.5 to 1.5
- up_hidden: bfloat16 [8, 16, 2048], P(None, None, 'tensor'), may hold values from -1.5 to 1.5
- up_router: bfloat16 [8, 16, 8], replicated, may hold values from -0.75 to 0.75
- down_heads: bfloat16 [8, 512, 16], P(None, 'tensor'), may hold values from -0.25 to 0.25
- down_hidden: bfloat16 [8, 2048, 16], P(None, 'tensor'), may hold values from -0.125 to 0.125
- up_attn_out: bfloat16 [8, 16, 512], replicated, may hold values from -6 to 6
- up_expert_out: bfloat16 [8, 16, 512], replicated, may hold values from -12 to 12
- routes: int32 [12608, 2], P('dp'), may hold values from 0 to 7, all different within a row
- priority: int32 [8, 1576], P('dp'), may hold values from 0 to 1575, each once within a row
- adapter_index: int32 [64], P('dp'), may hold values from 0 to 7
Outputs:
- block_out: float32 [12608, 512], P(('dp', 'tensor'))
- input_grad: float32 [12608, 512], P(('dp', 'tensor'))
- grad_down_in: float32 [5, 8, 512, 16], replicated
- grad_up_heads: float32 [3, 8, 16, 512], P(None, None, None, 'tensor')
- grad_up_hidden: float32 [8, 16, 2048], P(None, None, 'tensor')
- grad_up_router: float32 [8, 16, 8], replicated
- grad_down_heads: float32 [8, 512, 16], P(None, 'tensor')
- grad_down_hidden: float32 [8, 2048, 16], P(None, 'tensor')
- grad_up_attn_out: float32 [8, 16, 512], replicated
- grad_up_expert_out: float32 [8, 16, 512], replicated
Inputs may be any that keep to these rules, and one draw needn't show every extreme that they name: `routes`: each row names two different experts. `priority`: each row holds every number from 0 to 1575 once.
All inputs are finite; a program needn't handle non-finite values.
Results may differ from a plain program's by a relative error of at most 0.023.
The roundings to bfloat16 on the way count: a program that leaves them out, or rounds other values in their place, can miss the bound.
Values may be sent and summed in bfloat16 or wider, within the bound.
No kernel may reach another device: no remote copies, remote signals or barrier semaphores. Data moves between devices by JAX's collectives and lax.ppermute only.
A program may use at most 192 MiB of HBM per device.

v0:
```python
from functools import partial

import jax
import jax.numpy as jnp
from jax import lax
from jax.experimental import pallas as pl
from jax.experimental.pallas import tpu as pltpu
from jax.sharding import PartitionSpec as P

HEADS = 8
RANK = 16
ADAPTERS = 8
SEQ = 197
EXPERTS = 8
HEAD_DIM = 64
CAP = 394

EPS = 1e-06
CODE = ADAPTERS * RANK
ROWS = 208
UNIT = 16
SCALE = HEAD_DIM ** (-0.5)
F32 = jnp.float32
BF16 = jnp.bfloat16
MIB = 1024 * 1024


def dot(left, right):
    return lax.dot_general(left, right, (((1,), (0,)), ((), ())), preferred_element_type=F32)


def dot_t(left, right):
    return lax.dot_general(left, right, (((1,), (1,)), ((), ())), preferred_element_type=F32)


def tdot(left, right):
    return lax.dot_general(left, right, (((0,), (0,)), ((), ())), preferred_element_type=F32)


def lanes(shape):
    return lax.broadcasted_iota(jnp.int32, shape, len(shape) - 1)


def sublanes(shape):
    return lax.broadcasted_iota(jnp.int32, shape, len(shape) - 2)


def norm_rows(value, gain):
    center = value - jnp.mean(value, -1, keepdims=True)
    spread = jnp.mean(center * center, -1, keepdims=True)
    return center * lax.rsqrt(spread + EPS) * gain


def norm_back(value, gain, grad):
    center = value - jnp.mean(value, -1, keepdims=True)
    rate = lax.rsqrt(jnp.mean(center * center, -1, keepdims=True) + EPS)
    unit = center * rate
    grad = grad * gain
    along = jnp.mean(grad * unit, -1, keepdims=True)
    return rate * (grad - jnp.mean(grad, -1, keepdims=True) - unit * along)


def gelu_pair(value):
    square = value * value
    inner = 0.7978845608028654 * value * (1.0 + 0.044715 * square)
    bent = jnp.tanh(inner)
    half = 0.5 * (1.0 + bent)
    slope = half + 0.5 * value * (1.0 - bent * bent) * (
        0.7978845608028654 * (1.0 + 3.0 * 0.044715 * square)
    )
    return value * half, slope


def call(
    body, outs, scratch=(), smem=0, grid=None, in_specs=None, out_specs=None, cost=None, vmem=56
):
    options = {}
    if grid is not None:
        options = dict(grid=grid, in_specs=in_specs, out_specs=out_specs)
    elif smem:
        def build(*args):
            specs = [pl.BlockSpec(memory_space=pltpu.SMEM)] * smem
            specs += [pl.BlockSpec(memory_space=pltpu.VMEM)] * (len(args) - smem)
            return call(body, outs, scratch, 0, (), specs, None, cost, vmem)(*args)

        return build
    if grid == ():
        options = dict(in_specs=in_specs)
    return pl.pallas_call(
        body,
        out_shape=outs,
        scratch_shapes=list(scratch),
        compiler_params=pltpu.CompilerParams(vmem_limit_bytes=vmem * MIB),
        cost_estimate=cost,
        **options,
    )


def like(shape, dtype):
    return jax.ShapeDtypeStruct(shape, dtype)


def cost(micros):
    return pl.CostEstimate(
        flops=int(micros * 1.1e9), bytes_accessed=int(micros * 3.6e6), transcendentals=0
    )


def image_mask(adapter, index):
    return jnp.where(lanes((1, CODE)) // RANK == adapter[index], 1.0, 0.0)


def route_kernel(cot, rflat, rrow, prow, pcol, dy, place_out, table_out, wide):
    images = dy.shape[0] // ROWS
    chunks, unused, count = rrow.shape
    wide[...] = jnp.zeros_like(wide)
    wide[0 : cot.shape[0], :] = cot[...].astype(F32)
    for image in range(images):
        part = wide[image * SEQ : image * SEQ + ROWS, :]
        part = jnp.where(sublanes((ROWS, 1)) < SEQ, part, 0.0)
        dy[image * ROWS : (image + 1) * ROWS, :] = part.astype(BF16)
    kinds = sublanes((2 * EXPERTS, rflat.shape[1]))
    first = jnp.where(rflat[0:1, :] == kinds, 1.0, 0.0)
    second = jnp.where(rflat[1:2, :] == kinds, 1.0, 0.0)
    first_all = jnp.sum(first, axis=1, keepdims=True)
    first = first.astype(BF16)
    second = second.astype(BF16)
    kinds = sublanes((2 * EXPERTS, count))
    above = jnp.where(sublanes((count, count)) < lanes((count, count)), 1.0, 0.0).astype(BF16)
    square = (2 * EXPERTS, 2 * EXPERTS)
    below = jnp.where(lanes(square) < sublanes(square), 1.0, 0.0).astype(BF16)
    lane = lanes((2 * EXPERTS, 128))
    table = jnp.zeros((2 * EXPERTS, 128), F32)
    filled = jnp.zeros((2 * EXPERTS, 1), F32)
    for chunk in range(chunks):
        earlier = jnp.where(pcol[...] < prow[chunk], 1.0, 0.0).astype(BF16)
        is_first = rrow[chunk, 0:1, :] == kinds
        is_second = rrow[chunk, 1:2, :] == kinds
        place = jnp.where(is_first, dot(first, earlier), 1e9)
        place = jnp.where(is_second, dot(second, earlier) + first_all, place)
        kept = place < CAP
        held = jnp.where(kept, 1.0, 0.0)
        rank = dot(held.astype(BF16), above)
        units = jnp.sum(held, axis=1, keepdims=True)
        units = jnp.floor((units + (UNIT - 1)) * (1.0 / UNIT))
        start = dot(below, jnp.broadcast_to(units, (2 * EXPERTS, 128)).astype(BF16))[:, 0:1]
        spot = jnp.where(kept, start * UNIT + rank + 1.0, 0.0)
        place_out[chunk, 0:1, :] = (
            jnp.sum(jnp.where(is_first, spot, 0.0), axis=0, keepdims=True) - 1.0
        )
        place_out[chunk, 1:2, :] = (
            jnp.sum(jnp.where(is_second, spot, 0.0), axis=0, keepdims=True) - 1.0
        )
        table = jnp.where(lane == chunk, units, table)
        table = jnp.where(lane == chunks + chunk, start, table)
        table = jnp.where(lane == 2 * chunks + chunk, filled, table)
        filled = filled + units
    table = jnp.where(lane == 3 * chunks, filled, table)
    table_out[...] = table.astype(jnp.int32)


def assemble_kernel(count, *refs):
    parts, (extra, other_extra, out, ids) = refs[:count], refs[count:]
    feats = out.shape[2] // count
    out[0, 4] = extra[...]
    out[1, 4] = other_extra[...]
    for step, owner in enumerate(block_owners(count)):
        rows = pl.ds(pl.multiple_of(owner * feats, feats), feats)
        for side in range(2):
            for member in range(4):
                out[side, member, rows, :] = parts[step][
                    side, member * feats : (member + 1) * feats, :
                ]
        ids[owner] = parts[step][0, 4 * feats : 4 * feats + 16, :]


def forward_kernel(
    adapter, tokens, gain, mine, other, down, up_out,
    weights, x_out, normed_out, code_out, qkv_out, prob_out, mixed_out, hcode_out,
    middle_out, normed2_out, wide,
):
    me = lax.axis_index("tensor")
    for step in range(4):
        cols = pl.ds(pl.multiple_of(lax.bitwise_xor(me, step) * 128, 128), 128)
        weights[:, :, cols] = (mine, other)[step % 2][step // 2]
    images = x_out.shape[0] // ROWS
    width = tokens.shape[1]
    wide[...] = jnp.zeros_like(wide)
    wide[0 : tokens.shape[0], :] = tokens[...].astype(F32)
    for image in range(images):
        at = image * ROWS
        rows = slice(at, at + ROWS)
        mask = image_mask(adapter, me * images + image)
        real = sublanes((ROWS, 1)) < SEQ
        x = jnp.where(real, wide[image * SEQ : image * SEQ + ROWS, :], 0.0)
        x_out[rows, :] = x
        normed = norm_rows(x, gain[0:1, :]).astype(BF16)
        normed_out[rows, :] = normed
        for member in range(3):
            code = (mask * dot_t(normed, down[member])).astype(BF16)
            code_out[rows, member * CODE : (member + 1) * CODE] = code
            up = weights[4, member * CODE : (member + 1) * CODE, :]
            proj = dot(normed, weights[member]) + dot(code, up)
            qkv_out[rows, member * width : (member + 1) * width] = proj.astype(BF16)
        low_half = lanes((1, 128)) < HEAD_DIM
        half = (low_half, jnp.logical_not(low_half))
        real_key = lanes((1, ROWS)) < SEQ
        for pair in range(HEADS // 2):
            cols = pair * 128
            q = qkv_out[rows, cols : cols + 128].astype(F32) * SCALE
            k = qkv_out[rows, width + cols : width + cols + 128]
            v = qkv_out[rows, 2 * width + cols : 2 * width + cols + 128].astype(F32)
            mixed = jnp.zeros((ROWS, 128), F32)
            for head in range(2):
                score = dot_t(jnp.where(half[head], q, 0.0).astype(BF16), k)
                score = jnp.where(real_key, score, -1e30)
                raised = jnp.exp(score - jnp.max(score, -1, keepdims=True))
                prob = raised / jnp.sum(raised, -1, keepdims=True)
                prob_out[(image * HEADS // 2 + pair) * 2 + head] = prob
                mixed = mixed + dot(
                    prob.astype(BF16), jnp.where(half[head], v, 0.0).astype(BF16)
                )
            mixed_out[rows, cols : cols + 128] = mixed.astype(BF16)
        mixed = mixed_out[rows, :]
        hcode = (mask * dot_t(mixed, weights[4, 3 * CODE : 4 * CODE, :])).astype(BF16)
        hcode_out[rows, :] = hcode
        middle = x + dot_t(mixed, weights[3]) + dot(hcode, up_out[...])
        middle_out[rows, :] = middle
        normed2_out[rows, :] = norm_rows(middle, gain[1:2, :]).astype(BF16)


def row_adapters(adapter, chunk, count):
    images = count // ROWS
    which = jnp.zeros((count, 1), jnp.int32)
    for image in range(images):
        which = jnp.where(
            sublanes((count, 1)) // ROWS == image, adapter[chunk * images + image], which
        )
    return which


def move_units(table, chunk, expert, chunk_ref, expert_ref, forward):
    start = table[expert, 4 + chunk]
    target = table[expert, 8 + chunk]

    def move(unit, carry):
        here = pl.ds(pl.multiple_of((start + unit) * UNIT, UNIT), UNIT)
        there = pl.ds(pl.multiple_of((target + unit) * UNIT, UNIT), UNIT)
        if forward:
            expert_ref[there, :] = chunk_ref[here, :]
        else:
            chunk_ref[here, :] = expert_ref[there, :]
        return carry

    lax.fori_loop(0, table[expert, chunk], move, 0)


def clear_units(ref, start):
    def clear(unit, carry):
        rows = pl.ds(pl.multiple_of(unit * UNIT, UNIT), UNIT)
        ref[rows, :] = jnp.zeros((UNIT, ref.shape[1]), ref.dtype)
        return carry

    lax.fori_loop(start, ref.shape[0] // UNIT, clear, 0)


def dispatch_kernel(
    adapter, table, own, core, side, both, dy_own, dy_core, dy_side, dy_both,
    place, down, router, up_router,
    slots, normed_out, rcode_out, prob_out, rows, packed,
):
    me = lax.axis_index("tensor")
    count = own.shape[0]
    width = own.shape[1]
    lane = lanes((1, 128))
    for index, (part, dy) in enumerate(
        ((own, dy_own), (core, dy_core), (side, dy_side), (both, dy_both))
    ):
        normed_out[index] = part[...]
        rows[index, :, 0:width] = part[...]
        rows[index, :, width : 2 * width] = dy[...]

    def each(index, carry):
        chunk = lax.bitwise_xor(me, index)
        which = row_adapters(adapter, chunk, count)
        mask = jnp.where(lane // RANK == which, 1.0, 0.0)
        normed = rows[index, :, 0:width]
        rcode = (mask * dot_t(normed, down[4])).astype(BF16)
        rcode_out[index] = rcode
        logits = dot_t(normed, router[...]) + dot_t(rcode, up_router[...])
        logits = jnp.where(lane < 2 * EXPERTS, logits, -1e30)
        raised = jnp.exp(logits - jnp.max(logits, -1, keepdims=True))
        mass = jnp.sum(jnp.where(lane < EXPERTS, raised, 0.0), -1, keepdims=True)
        prob = raised / mass
        prob_out[index] = prob
        high = prob.astype(BF16).astype(F32)
        aux = jnp.where(lane < EXPERTS, high, prob - high)
        aux = jnp.where(lane < 2 * EXPERTS, aux, jnp.where(lane == 16 + which, 1.0, 0.0))
        rows[index, :, 2 * width : 2 * width + 128] = aux.astype(BF16)
        spot = sublanes((packed.shape[0], count)).astype(F32)
        chosen = jnp.logical_or(spot == place[chunk, 0:1, :], spot == place[chunk, 1:2, :])
        chosen = jnp.where(chosen, 1.0, 0.0).astype(BF16)
        packed[...] = dot(chosen, rows[index]).astype(BF16)

        def spread(expert, carry):
            move_units(table, chunk, expert, packed, slots.at[expert], True)
            return carry

        return lax.fori_loop(0, EXPERTS, spread, carry)

    lax.fori_loop(0, 4, each, 0)

    def clear(expert, carry):
        clear_units(slots.at[expert], table[expert, 12])
        return carry

    lax.fori_loop(0, EXPERTS, clear, 0)


def expert_body(expert, slots, w_in, w_out, up_hid, down_hid, up_exo, down, g_hid, g_exo, out):
    width = w_in.shape[0]
    lane = lanes((1, 128))
    x = slots[:, 0:width]
    dy = slots[:, width : 2 * width].astype(F32)
    aux = slots[:, 2 * width : 2 * width + 128]
    expand = jnp.where(sublanes((128, CODE)) - 16 == lanes((128, CODE)) // RANK, 1.0, 0.0)
    mask = dot(aux, expand.astype(BF16))
    here = jnp.logical_and(lax.rem(lane, EXPERTS) == expert, lane < 2 * EXPERTS)
    gate = jnp.sum(jnp.where(here, aux.astype(F32), 0.0), -1, keepdims=True)
    hcode = (mask * dot_t(x, down[3])).astype(BF16)
    before = dot(x, w_in[...]) + dot(hcode, up_hid[...])
    active, slope = gelu_pair(before)
    active = active.astype(BF16)
    ocode = (mask * dot_t(active, down_hid[...])).astype(BF16)
    returned = dot_t(active, w_out[...]) + dot(ocode, up_exo[...])
    gate_grad = jnp.sum(returned * dy, -1, keepdims=True)
    back = (gate * dy).astype(BF16)
    ocode_grad = (mask * dot_t(back, up_exo[...])).astype(BF16)
    active_grad = dot(back, w_out[...]) + dot(ocode_grad, down_hid[...])
    before_grad = (slope * active_grad).astype(BF16)
    hcode_grad = (mask * dot_t(before_grad, up_hid[...])).astype(BF16)
    x_grad = dot_t(before_grad, w_in[...]) + dot(hcode_grad, down[3])
    g_hid[0] += tdot(hcode, before_grad)
    g_hid[1] += tdot(ocode_grad, active)
    g_exo[0] += tdot(hcode_grad, x)
    g_exo[1] += tdot(ocode, back)
    high = gate_grad.astype(BF16).astype(F32)
    spread = jnp.where(here, jnp.where(lane < EXPERTS, high, gate_grad - high), 0.0)
    out[:, 0:width] = (gate * returned).astype(BF16)
    out[:, width : 2 * width] = x_grad.astype(BF16)
    out[:, 2 * width : 2 * width + 128] = spread.astype(BF16)


def fetch_weights(parts, joined, sems, step, count):
    owners = block_owners(min(len(parts), 8))
    feats = parts[0].shape[2]
    slot = lax.rem(step, 2)

    def copies(part, expert, slot, place):
        rows = pl.ds(pl.multiple_of(owners[place] * feats, feats), feats)
        return pltpu.make_async_copy(
            part.at[:, expert], joined.at[slot, :, rows, :], sems.at[slot, place]
        )

    def start(expert, slot):
        for place in range(len(owners) - 1):
            copies(parts[place], expert, slot, place).start()
        place = len(owners) - 1
        if len(parts) == len(owners):
            copies(parts[place], expert, slot, place).start()
            return
        half = parts[place].shape[1]

        @pl.when(expert < half)
        def _():
            copies(parts[place], expert, slot, place).start()

        @pl.when(expert >= half)
        def _():
            copies(parts[place + 1], expert - half, slot, place).start()

    @pl.when(step == 0)
    def _():
        start(0, 0)

    @pl.when(step + 1 < count)
    def _():
        start(step + 1, 1 - slot)

    for place in range(len(owners)):
        copies(parts[place], 0, slot, place).wait()
    return joined.at[slot, 0], joined.at[slot, 1]


def block_owners(size):
    me = lax.axis_index("dp")
    if size == 1:
        return (0,)
    owners = []
    for step in range(size // 2):
        owner = lax.rem(me - 2 * step + size, size)
        owners += [owner, lax.bitwise_xor(owner, 1)]
    return owners


def early_kernel(size, count, *refs):
    parts, refs = refs[:size], refs[size:]
    slots, up_hid, down_hid, up_exo, down, out, g_hid, g_exo, joined, sems = refs
    step = pl.program_id(0)

    @pl.when(step == 0)
    def _():
        g_hid[...] = jnp.zeros_like(g_hid)
        g_exo[...] = jnp.zeros_like(g_exo)

    w_in, w_out = fetch_weights(parts, joined, sems, step, count)
    expert_body(
        step, slots.at[0], w_in, w_out, up_hid, down_hid, up_exo, down,
        g_hid, g_exo, out.at[0],
    )


def late_kernel(size, base, *refs):
    parts, refs = refs[:size], refs[size:]
    (
        slots, up_hid, down_hid, up_exo, down, before, g_hid_before, g_exo_before,
        adapter, table, normed, rcode, prob, place, router, up_router,
        mix_keep, mix_send, grad_keep, grad_send, grads_out,
        joined, sems, late, g_hid, g_exo, g_router, packed,
    ) = refs
    step = pl.program_id(0)
    width = down.shape[2]
    lane = lanes((1, 128))

    @pl.when(step == 0)
    def _():
        g_hid[...] = g_hid_before[...]
        g_exo[...] = g_exo_before[...]
        g_router[...] = jnp.zeros_like(g_router)

    w_in, w_out = fetch_weights(parts, joined, sems, step, EXPERTS - base)
    expert_body(
        step + base, slots.at[0], w_in, w_out, up_hid, down_hid, up_exo, down,
        g_hid, g_exo, late.at[step],
    )

    @pl.when(step == pl.num_programs(0) - 1)
    def _():
        me = lax.axis_index("tensor")
        count = mix_keep.shape[1]

        def combine(index, mix_out, grad_out):
            chunk = lax.bitwise_xor(me, index)
            for base_expert, source in ((0, before), (base, late)):

                def collect(expert, carry):
                    move_units(
                        table, chunk, expert + base_expert, packed, source.at[expert], False
                    )
                    return carry

                lax.fori_loop(0, source.shape[0], collect, 0)
            ending = EXPERTS - 1
            clear_units(packed, table[ending, 4 + chunk] + table[ending, chunk])
            spot = lanes((count, packed.shape[0])).astype(F32)
            chosen = jnp.logical_or(
                spot == place[chunk, :, 0:1], spot == place[chunk, :, 1:2]
            )
            total = dot(jnp.where(chosen, 1.0, 0.0).astype(BF16), packed[...])
            mask = jnp.where(lane // RANK == row_adapters(adapter, chunk, count), 1.0, 0.0)
            mix_out[...] = total[:, 0:width].astype(BF16)
            gates = total[:, 2 * width : 2 * width + 128]
            probs = jnp.where(lane < 2 * EXPERTS, prob[index], 0.0)
            mean = jnp.sum(probs * gates, -1, keepdims=True)
            logit = (probs * (gates - jnp.where(lane < EXPERTS, mean, 0.0))).astype(BF16)
            rcode_grad = (mask * dot(logit, up_router[...])).astype(BF16)
            grad = total[:, width : 2 * width] + dot(logit, router[...])
            grad = grad + dot(rcode_grad, down[4])
            grad_out[...] = grad.astype(BF16)
            g_router[0] += tdot(rcode_grad, normed[index])
            g_router[1, :, 0:128] += tdot(logit, rcode[index])

        def pair(half, carry):
            combine(2 * half, mix_keep.at[half], grad_keep.at[half])
            combine(2 * half + 1, mix_send.at[half], grad_send.at[half])
            return carry

        lax.fori_loop(0, 2, pair, 0)
        shared = (g_exo.at[0], g_router.at[0], g_exo.at[1], g_router.at[1])
        if grads_out.dtype == F32:
            for member in range(4):
                grads_out[member] = shared[member][...]
            grads_out[4:6] = g_hid[...]
            return
        for owner in range(8):
            member, at = divmod(owner * 64, CODE)
            grads_out[owner, 0:64, :] = shared[member][at : at + 64, :].astype(BF16)
            member, at = divmod(owner * 32, CODE)
            grads_out[owner, 64:96, :] = g_hid[member, at : at + 32, :].astype(BF16)


def backward_kernel(
    adapter, dy, middle, grad_a, grad_b, grad_c, gain, weights, up_out,
    normed_in, code_in, qkv_in, prob_in, mixed_in, hcode_in,
    middle_grad_out, proj_grad, code_grad_out, grads_out, mixed_grad, whole,
):
    me = lax.axis_index("tensor")
    images = dy.shape[0] // ROWS
    width = dy.shape[1]
    compact = grads_out.shape[0] == 32

    def keep(image, member, grad):
        if not compact:
            grads_out[member] = grad if image == 0 else grads_out[member] + grad
            return
        whole[member] = grad
        start = pl.multiple_of(adapter[me * images + image] * RANK, RANK)
        rows = whole[member, pl.ds(start, RANK), :].astype(BF16)
        for block in range(4):
            grads_out[member * 4 + block, image * RANK : (image + 1) * RANK, :] = rows[
                :, block * 128 : (block + 1) * 128
            ]

    for image in range(images):
        at = image * ROWS
        rows = slice(at, at + ROWS)
        mask = image_mask(adapter, me * images + image)
        summed = grad_a[0, rows, :].astype(F32) + grad_b[0, rows, :].astype(F32)
        summed = summed + grad_c[rows, :].astype(F32)
        middle_grad = dy[rows, :].astype(F32) + norm_back(
            middle[rows, :], gain[1:2, :], summed
        )
        middle_grad_out[rows, :] = middle_grad
        low = middle_grad.astype(BF16)
        hcode_grad = (mask * dot_t(low, up_out[...])).astype(BF16)
        down_heads = weights[4, 3 * CODE : 4 * CODE, :]
        mixed_grad[...] = (dot(low, weights[3]) + dot(hcode_grad, down_heads)).astype(BF16)
        keep(image, 7, tdot(hcode_in[rows, :], low))
        keep(image, 3, tdot(hcode_grad, mixed_in[rows, :]))
        low_half = lanes((1, 128)) < HEAD_DIM
        half = (low_half, jnp.logical_not(low_half))
        for pair in range(HEADS // 2):
            cols = pair * 128
            q = qkv_in[rows, cols : cols + 128].astype(F32) * SCALE
            k = qkv_in[rows, width + cols : width + cols + 128].astype(F32) * SCALE
            v = qkv_in[rows, 2 * width + cols : 2 * width + cols + 128]
            m = mixed_grad[:, cols : cols + 128].astype(F32)
            q_grad = jnp.zeros((ROWS, 128), F32)
            k_grad = jnp.zeros((ROWS, 128), F32)
            v_grad = jnp.zeros((ROWS, 128), F32)
            for head in range(2):
                prob = prob_in[(image * HEADS // 2 + pair) * 2 + head]
                m_head = jnp.where(half[head], m, 0.0).astype(BF16)
                v_grad = v_grad + tdot(prob.astype(BF16), m_head)
                weight_grad = dot_t(m_head, v)
                along = jnp.sum(prob * weight_grad, -1, keepdims=True)
                score = (prob * (weight_grad - along)).astype(BF16)
                q_grad = q_grad + dot(score, jnp.where(half[head], k, 0.0).astype(BF16))
                k_grad = k_grad + tdot(score, jnp.where(half[head], q, 0.0).astype(BF16))
            proj_grad[rows, cols : cols + 128] = q_grad.astype(BF16)
            proj_grad[rows, width + cols : width + cols + 128] = k_grad.astype(BF16)
            proj_grad[rows, 2 * width + cols : 2 * width + cols + 128] = v_grad.astype(BF16)
        normed = normed_in[rows, :]
        for member in range(3):
            grad = proj_grad[rows, member * width : (member + 1) * width]
            up = weights[4, member * CODE : (member + 1) * CODE, :]
            code_grad = (mask * dot_t(grad, up)).astype(BF16)
            code_grad_out[rows, member * CODE : (member + 1) * CODE] = code_grad
            code = code_in[rows, member * CODE : (member + 1) * CODE]
            keep(image, member, tdot(code, grad))
            keep(image, 4 + member, tdot(code_grad, normed))


def early_sum_kernel(came, keep, send, hid):
    me = lax.axis_index("tensor")
    for index in range(4):
        start = pl.multiple_of(lax.bitwise_xor(me, index) * 16, 16)
        total = came[0, pl.ds(start, 16), :].astype(F32)
        for owner in range(1, came.shape[0]):
            total = total + came[owner, pl.ds(start, 16), :].astype(F32)
        (keep, send)[index % 2][index // 2] = total.astype(BF16)
    total = came[0, 64:96, :].astype(F32)
    for owner in range(1, came.shape[0]):
        total = total + came[owner, 64:96, :].astype(F32)
    hid[...] = total.astype(BF16)


def late_sum_kernel(came, ids, hid, rows_a, rows_b, rows_c, out):
    square = (CODE, CODE)
    total = jnp.zeros(square, F32)
    same = lax.rem(sublanes(square), RANK) == lax.rem(lanes(square), RANK)
    kind = (sublanes(square) // RANK).astype(F32)
    for owner in range(ids.shape[0]):
        chosen = jnp.logical_and(same, kind == ids[owner, 0:1, :].astype(F32))
        total = total + dot(jnp.where(chosen, 1.0, 0.0).astype(BF16), came[owner])
    total = total.astype(BF16)
    rows = rows_a[0].astype(F32) + rows_b[0].astype(F32) + rows_c[...].astype(F32)
    rows = rows.astype(BF16)
    for owner in range(out.shape[0]):
        out[owner, 0:32, :] = hid[...]
        out[owner, 32:48, :] = rows
        for slab in range(4):
            out[owner, 48:80, slab * 128 : (slab + 1) * 128] = total[
                slab * 32 : (slab + 1) * 32, :
            ]


def unpack_kernel(
    came, own, core, side, both,
    down_in, up_out, up_exo, router_out, heads, down_heads, up_hid, down_hid, router,
):
    me = lax.axis_index("tensor")
    for owner in range(8):
        member, at = divmod(owner * 32, CODE)
        (up_hid, down_hid)[member][at : at + 32, :] = came[owner, 0:32, :].astype(F32)
    for member in range(4):
        target = down_heads if member == 3 else heads.at[member]
        for slab in range(4):
            target[slab * 32 : (slab + 1) * 32, :] = came[
                member, 48:80, slab * 128 : (slab + 1) * 128
            ].astype(F32)
    late = (down_in.at[0], down_in.at[1], down_in.at[2], up_out)
    early = (down_in.at[3], down_in.at[4], up_exo, router)
    for index, part in enumerate((own, core, side, both)):
        spot = lax.bitwise_xor(me, index)
        cols = pl.ds(pl.multiple_of(spot * 128, 128), 128)
        for member in range(4):
            for slab in range(4):
                late[member][slab * 32 : (slab + 1) * 32, cols] = part[
                    member * 32 : (member + 1) * 32, slab * 128 : (slab + 1) * 128
                ].astype(F32)
        for owner in range(8):
            rows = pl.ds(pl.multiple_of((owner % 2) * 64 + spot * 16, 16), 16)
            early[owner // 2][rows, :] = part[
                128 + owner * 16 : 144 + owner * 16, :
            ].astype(F32)
    router_out[...] = router[0:EXPERTS, 0:CODE] + router[EXPERTS : 2 * EXPERTS, 0:CODE]


def input_kernel(
    middle_grad, proj_grad, code_grad, x_in, gain, weights, down, input_grad, wide
):
    images = middle_grad.shape[0] // ROWS
    width = middle_grad.shape[1]
    for image in range(images):
        at = image * ROWS
        rows = slice(at, at + ROWS)
        normed_grad = jnp.zeros((ROWS, width), F32)
        for member in range(3):
            grad = proj_grad[rows, member * width : (member + 1) * width]
            normed_grad = normed_grad + dot_t(grad, weights[member])
            code = code_grad[rows, member * CODE : (member + 1) * CODE]
            normed_grad = normed_grad + dot(code, down[member])
        wide[...] = middle_grad[rows, :] + norm_back(x_in[rows, :], gain[0:1, :], normed_grad)
        input_grad[image * SEQ : (image + 1) * SEQ, :] = wide[0:SEQ, :]


def finish_kernel(middle, part_a, part_b, part_c, out, wide):
    images = middle.shape[0] // ROWS
    for image in range(images):
        rows = slice(image * ROWS, (image + 1) * ROWS)
        part = part_a[0, rows, :].astype(F32) + part_b[0, rows, :].astype(F32)
        wide[...] = middle[rows, :] + (part + part_c[rows, :].astype(F32))
        out[image * SEQ : (image + 1) * SEQ, :] = wide[0:SEQ, :]


def swap(value, bit):
    size = lax.axis_size("tensor")
    return lax.ppermute(value, "tensor", [(at, at ^ bit) for at in range(size)])


def gather_four(value):
    core = swap(value, 1)
    side = swap(value, 2)
    return value, core, side, swap(side, 1)


def after(value, *others):
    return lax.optimization_barrier((value,) + others)[0]


def reduce_pair(keep, send):
    came = swap(send, 1)
    other = (keep[1].astype(F32) + came[1].astype(F32)).astype(BF16)
    return keep, came, swap(other, 2)


def gather_projections(shards, extra, ids, others):
    size = lax.axis_size("dp")
    feats = shards.shape[1]
    if size == 8 and feats % 16 == 0:
        block = jnp.concatenate([shards.reshape(-1, 128), ids], 0)
        ring = Ring(jnp.stack([block, swap(block, 2)]))
        begun = ()
        for step in range(size // 2 - 1):
            ring.step(*(others[1:] if step == 2 else ()))
            begun += (ring.done,)
        parts = ring.finish()
        others = others[:1]
        return begun, *call(
            partial(assemble_kernel, size),
            (like((2, 5, size * feats, 128), BF16), like((size,) + ids.shape, BF16)),
            cost=cost(2),
        )(*parts, after(extra, *others), swap(extra, 2))
    whole = lax.all_gather(shards, "dp", axis=1, tiled=True)
    whole = jnp.concatenate([whole, extra[None]], 0)
    return ((),) * 3, jnp.stack([whole, swap(whole, 2)]), ids[None]


class Ring:
    def __init__(self, block):
        self.size = lax.axis_size("dp")
        self.block, self.parts, self.done = block, [], ()

    def along(self, value):
        size = self.size
        return lax.ppermute(value, "dp", [(at, (at + 2) % size) for at in range(size)])

    def across(self, value):
        return lax.ppermute(value, "dp", [(at, at ^ 1) for at in range(self.size)])

    def step(self, *waits, across=()):
        block = after(self.block, *self.done, *waits)
        self.done = self.along(block), self.across(after(block, *across))
        self.parts += [block, self.done[1]]
        self.block = self.done[0]

    def finish(self, *waits, split=None):
        if split is None:
            block = after(self.block, *self.done, *waits)
            return self.parts + [block, self.across(block)]
        passed, crossed = (after(value, *waits) for value in self.done)
        halves = self.across(passed[:, :split]), self.along(crossed[:, split:])
        return self.parts + [passed, *halves]


class Whole:
    def __init__(self, block):
        self.parts = [lax.all_gather(block, "dp", axis=2, tiled=True)]
        self.done = ()

    def step(self, *waits, across=()):
        pass

    def finish(self, *waits, split=None):
        return self.parts


def per_device(
    tokens,
    cotangent,
    norm_gain,
    qkv_weight,
    out_weight,
    expert_in,
    expert_out,
    router_weight,
    down_in,
    up_heads,
    up_hidden,
    up_router,
    down_heads,
    down_hidden,
    up_attn_out,
    up_expert_out,
    routes,
    priority,
    adapter_index,
):
    width = tokens.shape[1]
    local = tokens.shape[0]
    images = local // SEQ
    group_images = routes.shape[0] // SEQ
    count = images * ROWS
    tall = group_images * ROWS
    hidden = expert_in.shape[2]
    dp = lax.axis_size("dp")
    tensor = lax.axis_size("tensor")

    block = jnp.concatenate([qkv_weight, out_weight[None]], 0)
    ids = jnp.repeat(adapter_index.astype(BF16), CODE // adapter_index.shape[0])
    ids = jnp.broadcast_to(ids[None], (16, CODE))
    extra = jnp.concatenate(
        [
            up_heads.reshape(3 * CODE, up_heads.shape[3]),
            down_heads.swapaxes(1, 2).reshape(CODE, down_heads.shape[1]),
        ],
        0,
    )
    base = EXPERTS // 2
    fits = dp == 8 and expert_in.shape[1] % 16 == 0
    gather = Ring if fits else Whole
    early_ring = gather(jnp.stack([expert_in[:base], expert_out[:base]]))
    early_ring.step()
    late_block = jnp.stack([expert_in[base:], expert_out[base:]])

    down = down_in.swapaxes(2, 3).reshape(5, CODE, width)
    down_hid = down_hidden.swapaxes(1, 2).reshape(CODE, hidden)
    up_hid = up_hidden.reshape(CODE, hidden)
    up_out = up_attn_out.reshape(CODE, width)
    up_exo = up_expert_out.reshape(CODE, width)
    router = jnp.pad(jnp.tile(router_weight.T, (2, 1)), ((0, 128 - 2 * EXPERTS), (0, 0)))
    router_up = up_router.transpose(2, 0, 1).reshape(EXPERTS, CODE)
    router_up = jnp.pad(jnp.tile(router_up, (2, 1)), ((0, 128 - 2 * EXPERTS), (0, 0)))

    spare = ROWS - SEQ
    route_row = jnp.pad(
        routes.T.reshape(2, group_images, SEQ), ((0, 0), (0, 0), (0, spare)), constant_values=-1
    ).reshape(2, tall)
    rank_row = jnp.pad(
        priority.reshape(group_images, SEQ), ((0, 0), (0, spare)), constant_values=1 << 20
    ).reshape(1, tall)
    chunk_units = (2 * count + EXPERTS * (UNIT - 1)) // UNIT
    expert_units = -(-CAP // UNIT) + 4
    by_chunk = lambda value: value.reshape(-1, tensor, count).swapaxes(0, 1)
    dy, place, table = call(
        route_kernel,
        (
            like((count, width), BF16),
            like((tensor, 2, count), F32),
            like((2 * EXPERTS, 128), jnp.int32),
        ),
        scratch=[pltpu.VMEM((count, width), F32)],
        cost=cost(5),
    )(cotangent, route_row, by_chunk(route_row), by_chunk(rank_row), rank_row.T)
    dy_four = gather_four(dy)
    begun, mine, ids = gather_projections(block, extra, ids, (dy_four[2],) + early_ring.done)
    early_ring.step(*begun[1])
    late_ring = gather(after(late_block, *begun[2]))
    late_ring.step()
    other = swap(mine, 1)

    (
        weights, x, normed, code, qkv, prob, mixed, hcode, middle, normed2,
    ) = call(
        forward_kernel,
        (
            like((5, width, width), BF16),
            like((count, width), F32),
            like((count, width), BF16),
            like((count, 3 * CODE), BF16),
            like((count, 3 * width), BF16),
            like((images * HEADS, ROWS, ROWS), F32),
            like((count, width), BF16),
            like((count, CODE), BF16),
            like((count, width), F32),
            like((count, width), BF16),
        ),
        scratch=[pltpu.VMEM((count, width), F32)],
        smem=1,
        cost=cost(10),
        vmem=56,
    )(adapter_index, tokens, norm_gain, mine, other, down, up_out)

    normed2_four = gather_four(normed2)
    normed2_four = (after(normed2, *early_ring.done),) + normed2_four[1:]
    early_ring.step(normed2)
    late_ring.step(normed2_four[2])
    row_wide = 2 * width + 128
    chunk_slots = chunk_units * UNIT
    expert_slots = expert_units * UNIT
    slots, rows, rcode, probs = call(
        dispatch_kernel,
        (
            like((EXPERTS, expert_slots, row_wide), BF16),
            like((tensor, count, width), BF16),
            like((tensor, count, CODE), BF16),
            like((tensor, count, 128), F32),
        ),
        scratch=[
            pltpu.VMEM((tensor, count, row_wide), BF16),
            pltpu.VMEM((chunk_slots, row_wide), BF16),
        ],
        smem=2,
        cost=cost(17),
    )(adapter_index, table, *normed2_four, *dy_four, place, down, router, router_up)

    early_parts = early_ring.finish(slots, split=base // 2)
    ready = late_ring.done
    late_ring.step(slots, across=early_parts[7:])
    whole = lambda *shape: pl.BlockSpec(shape, lambda step: (0,) * len(shape))
    smem = pl.BlockSpec(memory_space=pltpu.SMEM)
    size = len(early_parts)
    shard = pl.BlockSpec(memory_space=pltpu.HBM)
    joined = [
        pltpu.VMEM((2, 2, width, hidden), BF16),
        pltpu.SemaphoreType.DMA((2, min(size, 8))),
    ]
    small = [
        whole(CODE, hidden), whole(CODE, hidden), whole(CODE, width), whole(5, CODE, width),
    ]
    early_out, g_hid, g_exo = call(
        partial(early_kernel, size, base),
        (
            like((base, expert_slots, row_wide), BF16),
            like((2, CODE, hidden), F32),
            like((2, CODE, width), F32),
        ),
        scratch=joined,
        grid=(base,),
        in_specs=[shard] * size
        + [pl.BlockSpec((1, expert_slots, row_wide), lambda step: (step, 0, 0))]
        + small,
        out_specs=(
            pl.BlockSpec((1, expert_slots, row_wide), lambda step: (step, 0, 0)),
            whole(2, CODE, hidden),
            whole(2, CODE, width),
        ),
        cost=cost(16),
    )(*early_parts, after(slots, *ready), up_hid, down_hid, up_exo, down)
    late_parts = late_ring.finish(early_out, split=base // 2)
    half = like((2, count, width), BF16)
    compact = dp == 8 and images == 2 and hidden == width == 512
    (
        mix_keep, mix_send, grad_keep, grad_send, early,
    ) = call(
        partial(late_kernel, size, base),
        (
            half, half, half, half,
            like((8, 96, width), BF16) if compact else like((6, CODE, width), F32),
        ),
        scratch=joined
        + [
            pltpu.VMEM((EXPERTS - base, expert_slots, row_wide), BF16),
            pltpu.VMEM((2, CODE, hidden), F32),
            pltpu.VMEM((2, CODE, width), F32),
            pltpu.VMEM((2, CODE, width), F32),
            pltpu.VMEM((chunk_slots, row_wide), BF16),
        ],
        grid=(EXPERTS - base,),
        in_specs=[shard] * size
        + [pl.BlockSpec((1, expert_slots, row_wide), lambda step: (step + base, 0, 0))]
        + small
        + [
            whole(base, expert_slots, row_wide),
            whole(2, CODE, hidden),
            whole(2, CODE, width),
            smem,
            smem,
            whole(tensor, count, width),
            whole(tensor, count, CODE),
            whole(tensor, count, 128),
            whole(tensor, count, 2),
            whole(128, width),
            whole(128, CODE),
        ],
        out_specs=(
            whole(2, count, width), whole(2, count, width),
            whole(2, count, width), whole(2, count, width),
            whole(8, 96, width) if compact else whole(6, CODE, width),
        ),
        cost=cost(30),
    )(
        *late_parts, slots, up_hid, down_hid, up_exo, down, early_out, g_hid, g_exo,
        adapter_index, table, rows, rcode, probs, place.swapaxes(1, 2), router, router_up,
    )

    both = ("dp", "tensor")
    if compact:
        early = lax.all_to_all(early, "dp", 0, 0)
    grads = reduce_pair(grad_keep, grad_send)
    mixes = reduce_pair(mix_keep, after(mix_send, grads[2]))

    middle_grad, proj_grad, code_grad, late = call(
        backward_kernel,
        (
            like((count, width), F32),
            like((count, 3 * width), BF16),
            like((count, 3 * CODE), BF16),
            like((32, images * RANK, 128), BF16) if compact else like((8, CODE, width), F32),
        ),
        scratch=[pltpu.VMEM((ROWS, width), BF16), pltpu.VMEM((8, CODE, width), F32)],
        smem=1,
        cost=cost(11),
        vmem=56,
    )(
        adapter_index, dy, middle, *grads, norm_gain, weights, up_out,
        normed, code, qkv, prob, mixed, hcode,
    )
    if compact:
        came = lax.all_to_all(late, both, 0, 0)
    input_grad = call(
        input_kernel,
        like((local, width), F32),
        scratch=[pltpu.VMEM((ROWS, width), F32)],
        cost=cost(5),
        vmem=56,
    )(middle_grad, proj_grad, code_grad, x, norm_gain, weights, down)
    block_out = call(
        finish_kernel,
        like((local, width), F32),
        scratch=[pltpu.VMEM((ROWS, width), F32)],
        cost=cost(2),
    )(after(middle, late), *mixes)

    if compact:
        keep = like((2, 16, width), BF16)
        keep, send, early_hid = call(
            early_sum_kernel, (keep, keep, like((32, width), BF16)), cost=cost(2)
        )(after(early, late))
        sums = reduce_pair(keep, send)
        packed = call(late_sum_kernel, like((dp, 80, width), BF16), cost=cost(2))(
            came.reshape(dp, CODE, 128), ids, early_hid, *sums
        )
        came = lax.all_to_all(packed, "dp", 0, 0)
        came = after(came, input_grad, block_out)
        mine = jnp.concatenate(
            [came[4:, 48:].reshape(128, width), came[:, 32:48].reshape(128, width)], 0
        )
        whole = like((CODE, width), F32)
        (
            grad_down_in, grad_up_out, grad_up_exo, router_grad,
            grad_up_heads, grad_down_heads, grad_up_hidden, grad_down_hidden,
        ) = call(
            unpack_kernel,
            (
                like((5, CODE, width), F32), whole, whole, like((EXPERTS, CODE), F32),
                like((3, CODE, 128), F32), like((CODE, 128), F32), whole, whole,
            ),
            scratch=[pltpu.VMEM((CODE, width), F32)],
            cost=cost(3),
        )(came, *gather_four(mine))
    else:
        cols = width // tensor
        early_shared = lax.psum(early[:4], both)
        early_hid = lax.psum(early[4:], "dp")
        late = lax.psum(late, both)
        late_heads = lax.dynamic_slice_in_dim(
            late[:4], lax.axis_index("tensor") * cols, cols, 2
        )
        grad_down_in = jnp.concatenate([late[4:7], early_shared[:2]], 0)
        grad_up_out, grad_up_exo = late[7], early_shared[2]
        router_grad = early_shared[3, :, :CODE]
        router_grad = router_grad[:EXPERTS] + router_grad[EXPERTS : 2 * EXPERTS]
        grad_up_heads, grad_down_heads = late_heads[:3], late_heads[3]
        grad_up_hidden, grad_down_hidden = early_hid[0], early_hid[1]
    split_up = lambda value: value.reshape(value.shape[:-2] + (ADAPTERS, RANK, value.shape[-1]))
    split_down = lambda value: split_up(value).swapaxes(-1, -2)
    grad_down_in = split_down(grad_down_in)
    grad_up_out = split_up(grad_up_out)
    grad_up_exo = split_up(grad_up_exo)
    grad_up_router = router_grad.reshape(EXPERTS, ADAPTERS, RANK).transpose(1, 2, 0)
    grad_up_heads = split_up(grad_up_heads)
    grad_down_heads = split_down(grad_down_heads)
    grad_up_hidden = split_up(grad_up_hidden)
    grad_down_hidden = split_down(grad_down_hidden)
    return (
        block_out,
        input_grad,
        grad_down_in,
        grad_up_heads,
        grad_up_hidden,
        grad_up_router,
        grad_down_heads,
        grad_down_hidden,
        grad_up_out,
        grad_up_exo,
    )


def solution(mesh):
    placed = (
        P(("dp", "tensor"), None),
        P(("dp", "tensor"), None),
        P(),
        P(None, "dp", "tensor"),
        P("dp", "tensor"),
        P(None, "dp", "tensor"),
        P(None, "dp", "tensor"),
        P(),
        P(),
        P(None, None, None, "tensor"),
        P(None, None, "tensor"),
        P(),
        P(None, "tensor", None),
        P(None, "tensor", None),
        P(),
        P(),
        P("dp", None),
        P("dp", None),
        P("dp"),
    )
    return jax.shard_map(
        per_device,
        mesh=mesh,
        in_specs=placed,
        out_specs=(
            P(("dp", "tensor"), None),
            P(("dp", "tensor"), None),
            P(),
            P(None, None, None, "tensor"),
            P(None, None, "tensor"),
            P(),
            P(None, "tensor", None),
            P(None, "tensor", None),
            P(),
            P(),
        ),
        check_vma=False,
    )
```

profile of v0, /device:TPU:0, one launch (start us, length us, event | category | flops | bytes accessed | tf_op | source)
XLA Modules:
  0.0 253.2 jit_solution(6092927683341107095)
XLA Ops:
  2.3 3.0 %collective-permute-start = (bf16[272,128]{1,0:T(8,128)(2,1)S(1)}, bf16[272,128]{1,0:T(8,128)(2,1)S(1)}, u32[]{:S(2)}, u32[]{:S(2)}) collective-permute-start(bf16[272,128]{1,0:T(8,128)(2,1)S(1)} %get-tuple-element.139), channel_id=1, source_target_pairs={{0,2},{1,3},{2,0},{3,1},{4,6},{5,7},{6,4},{7,5},{8,10},{9,11},{10,... | collective-permute-start | bytes 208904 | tf_op jit(solution)/shard_map/ppermute | solution.py:669
  5.4 2.3 collective-permute-done
  7.7 2.1 collective-permute-start.2
  21.5 5.0 %shard_map.258 = (bf16[416,512]{1,0:T(8,128)(2,1)}, f32[4,2,416]{2,1,0:T(2,128)}, s32[16,128]{1,0:T(8,128)}) custom-call(bf16[394,512]{1,0:T(8,128)(2,1)} %cot.1, s32[2,1664]{1,0:T(2,128)} %reshape.111.rflat, s32[4,2,416]{2,1,0:T(2,128)} %bitcast.73, s32[4,1,416]{2,1,0:T(1,128)} %transpose_reshape_reshape.3.prow, s32[1664,1]{1,0:T(8,128)} %transpose_reshape.4.pcol), custom_call_target="tpu_custom_call" | custom-call | flops 5500000256 | bytes 18000000 | tf_op jit(solution)/shard_map/pallas_call | solution.py:816
  32.3 2.3 collective-permute-done.7.refs_5_
  34.6 3.2 %collective-permute-done.8.refs_6_ = bf16[2,272,128]{2,1,0:T(8,128)(2,1)S(1)} collective-permute-done((bf16[2,272,128]{2,1,0:T(8,128)(2,1)S(1)}, bf16[2,272,128]{2,1,0:T(8,128)(2,1)S(1)}, u32[]{:S(2)}, u32[]{:S(2)}) %collective-permute-start.8) | collective-permute-done | bytes 139296 | tf_op jit(solution)/shard_map/ppermute | solution.py:717
  40.1 3.4 %collective-permute-done.11.refs_9_ = bf16[512,128]{1,0:T(8,128)(2,1)S(1)} collective-permute-done((bf16[512,128]{1,0:T(8,128)(2,1)S(1)}, bf16[512,128]{1,0:T(8,128)(2,1)S(1)}, u32[]{:S(2)}, u32[]{:S(2)}) %collective-permute-start.11) | collective-permute-done | bytes 131104 | tf_op jit(solution)/shard_map/ppermute | solution.py:669
  44.8 2.5 %shard_map.259 = (bf16[2,5,512,128]{3,2,1,0:T(8,128)(2,1)}, bf16[8,16,128]{2,1,0:T(8,128)(2,1)}) custom-call(bf16[2,272,128]{2,1,0:T(8,128)(2,1)} %copy-done.11, bf16[2,272,128]{2,1,0:T(8,128)(2,1)} %copy-done.48, bf16[2,272,128]{2,1,0:T(8,128)(2,1)} %copy-done.47, bf16[2,272,128]{2,1,0:T(8,128)(2,1)} %copy-done.50, bf16[2,272,128]{2,1,0:T(8,128)(2,1)} %copy-done.49, ...), custom_call_target="tpu_custom_call" | custom-call | flops 2200000000 | bytes 7200000 | tf_op jit(solution)/shard_map/pallas_call | solution.py:700
  51.7 9.7 %shard_map.260 = (bf16[5,512,512]{2,1,0:T(8,128)(2,1)}, f32[416,512]{1,0:T(8,128)}, bf16[416,512]{1,0:T(8,128)(2,1)}, bf16[416,384]{1,0:T(8,128)(2,1)}, bf16[416...) custom-call(s32[8]{0:T(128)} %adapter.5, ...), custom_call_target="tpu_custom_call" | custom-call | flops 11000000512 | bytes 36000000 | tf_op jit(solution)/shard_map/pallas_call | solution.py:84
  63.6 9.5 %collective-permute-done.13.refs_1_ = bf16[2,4,64,512]{3,2,1,0:T(8,128)(2,1)S(1)} collective-permute-done((bf16[2,4,64,512]{3,2,1,0:T(8,128)(2,1)S(1)}, bf16[2,4,64,512]{3,2,1,0:T(8,128)(2,1)S(1)}, u32[]{:S(2)}, u32[]{:S(2)}) %collective-permute-start.13) | collective-permute-done | bytes 524320 | tf_op jit(solution)/shard_map/ppermute | solution.py:720
  74.9 3.5 %collective-permute-done.14.refs_2_ = bf16[2,4,64,512]{3,2,1,0:T(8,128)(2,1)S(1)} collective-permute-done((bf16[2,4,64,512]{3,2,1,0:T(8,128)(2,1)S(1)}, bf16[2,4,64,512]{3,2,1,0:T(8,128)(2,1)S(1)}, u32[]{:S(2)}, u32[]{:S(2)}) %collective-permute-start.14) | collective-permute-done | bytes 524320 | tf_op jit(solution)/shard_map/ppermute | solution.py:717
  81.4 17.1 %shard_map.261 = (bf16[8,464,1152]{2,1,0:T(8,128)(2,1)}, bf16[4,416,512]{2,1,0:T(8,128)(2,1)}, bf16[4,416,128]{2,1,0:T(8,128)(2,1)}, f32[4,416,128]{2,1,0:T(8,128)}) custom-call(s32[8]{0:T(128)} %adapter.5, s32[16,128]{1,0:T(8,128)} %get-tuple-element.82.table.refs_18_, bf16[416,512]{1,0:T(8,128)(2,1)} %get-tuple-element.84.own, ...), custom_call_target="tpu_custom_call" | custom-call | flops 18699999232 | bytes 61200000 | tf_op jit(solution)/shard_map/pallas_call | solution.py:84
  101.5 2.6 %collective-permute-done.16.refs_3_ = bf16[2,4,64,512]{3,2,1,0:T(8,128)(2,1)S(1)} collective-permute-done((bf16[2,4,64,512]{3,2,1,0:T(8,128)(2,1)S(1)}, bf16[2,4,64,512]{3,2,1,0:T(8,128)(2,1)S(1)}, u32[]{:S(2)}, u32[]{:S(2)}) %collective-permute-start.16) | collective-permute-done | bytes 524320 | tf_op jit(solution)/shard_map/ppermute | solution.py:720
  104.1 2.2 collective-permute-done.17.refs_4_
  106.3 5.6 %collective-permute-done.27.refs_8_ = bf16[2,2,64,512]{3,2,1,0:T(8,128)(2,1)S(1)} collective-permute-done((bf16[2,2,64,512]{3,2,1,0:T(8,128)(2,1)S(1)}, bf16[2,2,64,512]{3,2,1,0:T(8,128)(2,1)S(1)}, u32[]{:S(2)}, u32[]{:S(2)}) %collective-permute-start.27) | collective-permute-done | bytes 262176 | tf_op jit(solution)/shard_map/ppermute | solution.py:717
  113.4 17.1 %shard_map.262 = (bf16[4,464,1152]{2,1,0:T(8,128)(2,1)}, f32[2,128,512]{2,1,0:T(8,128)}, f32[2,128,512]{2,1,0:T(8,128)}) custom-call(bf16[2,4,64,512]{3,2,1,0:T(8,128)(2,1)} %copy-done.4, bf16[2,4,64,512]{3,2,1,0:T(8,128)(2,1)} %copy-done.26, bf16[2,4,64,512]{3,2,1,0:T(8,128)(2,1)} %copy-done.25, bf16[2,4,64,512]{3,2,1,0:T(8,128)(2,1)} %collective-permute-done.19.refs_3_, ...), custom_call_target="tpu_custom_call" | custom-call | flops 17600000000 | bytes 57600000 | tf_op jit(solution)/shard_map/pallas_call | solution.py:892
  132.9 4.1 %collective-permute-done.30.refs_7_ = bf16[2,2,64,512]{3,2,1,0:T(8,128)(2,1)S(1)} collective-permute-done((bf16[2,2,64,512]{3,2,1,0:T(8,128)(2,1)S(1)}, bf16[2,2,64,512]{3,2,1,0:T(8,128)(2,1)S(1)}, u32[]{:S(2)}, u32[]{:S(2)}) %collective-permute-start.30) | collective-permute-done | bytes 262176 | tf_op jit(solution)/shard_map/ppermute | solution.py:720
  137.0 2.8 %collective-permute-done.31.refs_8_ = bf16[2,2,64,512]{3,2,1,0:T(8,128)(2,1)S(1)} collective-permute-done((bf16[2,2,64,512]{3,2,1,0:T(8,128)(2,1)S(1)}, bf16[2,2,64,512]{3,2,1,0:T(8,128)(2,1)S(1)}, u32[]{:S(2)}, u32[]{:S(2)}) %collective-permute-start.31) | collective-permute-done | bytes 262176 | tf_op jit(solution)/shard_map/ppermute | solution.py:717
  140.5 32.2 %shard_map.263 = (bf16[2,416,512]{2,1,0:T(8,128)(2,1)}, bf16[2,416,512]{2,1,0:T(8,128)(2,1)}, bf16[2,416,512]{2,1,0:T(8,128)(2,1)}, bf16[2,416,512]{2,1,0:T(8,128)(2,1)}, bf16[8,96,512]{2,1,0:T(8,128)(2,1)}) custom-call(bf16[2,4,64,512]{3,2,1,0:T(8,128)(2,1)} %copy-done.5, bf16[2,4,64,512]{3,2,1,0:T(8,128)(2,1)} %copy-done.27, ...), custom_call_target="tpu_custom_call" | custom-call | flops 32999999488 | bytes 108000000 | tf_op jit(solution)/shard_map/pallas_call | solution.py:916
  172.8 2.6 %collective-permute-done.32.grad_b = bf16[2,416,512]{2,1,0:T(8,128)(2,1)S(1)} collective-permute-done((bf16[2,416,512]{2,1,0:T(8,128)(2,1)}, bf16[2,416,512]{2,1,0:T(8,128)(2,1)S(1)}, u32[]{:S(2)}, u32[]{:S(2)}) %collective-permute-start.32) | collective-permute-done | bytes 852000 | tf_op jit(solution)/shard_map/ppermute | solution.py:669
  177.3 3.8 %all-to-all-start.1 = ((bf16[8,96,512]{2,1,0:T(8,128)(2,1)}), bf16[8,96,512]{2,1,0:T(8,128)(2,1)S(1)}, u32[]{:S(2)}, u32[]{:S(2)}) async-start(bf16[8,96,512]{2,1,0:T(8,128)(2,1)} %get-tuple-element.120), calls=%async_computation.1 | async-start | bytes 1572864 | tf_op jit(solution)/shard_map/all_to_all | solution.py:960
  181.2 7.5 %collective-permute-done.33.grad_c = bf16[416,512]{1,0:T(8,128)(2,1)S(1)} collective-permute-done((bf16[416,512]{1,0:T(8,128)(2,1)S(1)}, bf16[416,512]{1,0:T(8,128)(2,1)S(1)}, u32[]{:S(2)}, u32[]{:S(2)}) %collective-permute-start.33) | collective-permute-done | bytes 426016 | tf_op jit(solution)/shard_map/ppermute | solution.py:669
  189.5 11.6 %shard_map.264 = (f32[416,512]{1,0:T(8,128)}, bf16[416,1536]{1,0:T(8,128)(2,1)}, bf16[416,384]{1,0:T(8,128)(2,1)}, bf16[32,32,128]{2,1,0:T(8,128)(2,1)}) custom-call(s32[8]{0:T(128)} %adapter.5, bf16[416,512]{1,0:T(8,128)(2,1)} %get-tuple-element.75.dy_own.dy, f32[416,512]{1,0:T(8,128)} %get-tuple-element.111.middle, ...), custom_call_target="tpu_custom_call" | custom-call | flops 12099999744 | bytes 39600000 | tf_op jit(solution)/shard_map/pallas_call | solution.py:84
  201.3 3.6 %all-to-all-start = ((bf16[32,32,128]{2,1,0:T(8,128)(2,1)}), bf16[32,32,128]{2,1,0:T(8,128)(2,1)S(1)}, u32[]{:S(2)}, u32[]{:S(2)}) async-start(bf16[32,32,128]{2,1,0:T(8,128)(2,1)} %get-tuple-element.110), calls=%async_computation | async-start | bytes 524288 | tf_op jit(solution)/shard_map/all_to_all | solution.py:981
  213.0 2.5 all-to-all-done
  216.2 2.2 shard_map.268
  218.4 3.5 %all-to-all-start.2 = ((bf16[8,80,512]{2,1,0:T(8,128)(2,1)}), bf16[8,80,512]{2,1,0:T(8,128)(2,1)S(1)}, u32[]{:S(2)}, u32[]{:S(2)}) async-start(bf16[8,80,512]{2,1,0:T(8,128)(2,1)} %shard_map.268), calls=%async_computation.2 | async-start | bytes 1310720 | tf_op jit(solution)/shard_map/all_to_all | solution.py:1005
  223.3 5.4 %shard_map.266 = f32[394,512]{1,0:T(8,128)} custom-call(f32[416,512]{1,0:T(8,128)} %get-tuple-element.115.middle_grad, bf16[416,1536]{1,0:T(8,128)(2,1)} %get-tuple-element.116.proj_grad, bf16[416,384]{1,0:T(8,128)(2,1)} %get-tuple-element.117.code_grad, f32[416,512]{1,0:T(8,128)} %get-tuple-element.118.x_in, f32[2,512]{1,0:T(2,128)} %gain.5, ...), custom_call_target="tpu_custom_call" | custom-call | flops 5500000256 | bytes 18000000 | tf_op jit(solution)/shard_map/pallas_call | solution.py:982
  228.7 5.1 %collective-permute-done.35.part_c = bf16[416,512]{1,0:T(8,128)(2,1)S(1)} collective-permute-done((bf16[416,512]{1,0:T(8,128)(2,1)S(1)}, bf16[416,512]{1,0:T(8,128)(2,1)S(1)}, u32[]{:S(2)}, u32[]{:S(2)}) %collective-permute-start.35) | collective-permute-done | bytes 426016 | tf_op jit(solution)/shard_map/ppermute | solution.py:669
  234.5 3.0 %shard_map.265 = f32[394,512]{1,0:T(8,128)} custom-call(f32[416,512]{1,0:T(8,128)} %get-tuple-element.111.middle, bf16[2,416,512]{2,1,0:T(8,128)(2,1)} %get-tuple-element.112.part_a, bf16[2,416,512]{2,1,0:T(8,128)(2,1)} %copy-done.9, bf16[416,512]{1,0:T(8,128)(2,1)} %copy-done.39), custom_call_target="tpu_custom_call" | custom-call | flops 2200000000 | bytes 7200000 | tf_op jit(solution)/shard_map/pallas_call | solution.py:989
  240.5 6.1 %collective-permute-done.39.side = bf16[256,512]{1,0:T(8,128)(2,1)S(1)} collective-permute-done((bf16[256,512]{1,0:T(8,128)(2,1)S(1)}, bf16[256,512]{1,0:T(8,128)(2,1)S(1)}, u32[]{:S(2)}, u32[]{:S(2)}) %collective-permute-start.39) | collective-permute-done | bytes 262176 | tf_op jit(solution)/shard_map/ppermute | solution.py:669
  248.9 2.9 %shard_map.269 = (f32[5,128,512]{2,1,0:T(8,128)}, f32[128,512]{1,0:T(8,128)}, f32[128,512]{1,0:T(8,128)}, f32[8,128]{1,0:T(8,128)}, f32[3,128,128]{2,1,0:T(8,128...) custom-call(bf16[8,80,512]{2,1,0:T(8,128)(2,1)} %copy-done.2, bf16[256,512]{1,0:T(8,128)(2,1)} %copy-done.7, ...), custom_call_target="tpu_custom_call" | custom-call | flops 3300000000 | bytes 10800000 | tf_op jit(solution)/shard_map/pallas_call | solution.py:1014
  (220 shorter events, 61.8 us)
Async XLA Ops:
  7.7 10.7 %collective-permute-start.2 = (bf16[2,272,128]{2,1,0:T(8,128)(2,1)S(1)}, bf16[2,272,128]{2,1,0:T(8,128)(2,1)S(1)}, u32[]{:S(2)}, u32[]{:S(2)}) collective-permute-start(bf16[2,272,128]{2,1,0:T(8,128)(2,1)S(1)} %pad_maximum_fusion.3.refs_0_), channel_id=1, source_target_pairs={{0,8},{4,12},{8,16},{12,20},{16,24},{20,28},{24,0},{28,4},{1,9},{5... | collective-permute-start | bytes 417800 | tf_op jit(solution)/shard_map/ppermute | solution.py:717
  9.8 8.5 %collective-permute-start.1 = (bf16[2,272,128]{2,1,0:T(8,128)(2,1)S(1)}, bf16[2,272,128]{2,1,0:T(8,128)(2,1)S(1)}, u32[]{:S(2)}, u32[]{:S(2)}) collective-permute-start(bf16[2,272,128]{2,1,0:T(8,128)(2,1)S(1)} %pad_maximum_fusion.3.refs_0_), channel_id=1, source_target_pairs={{0,4},{4,0},{8,12},{12,8},{16,20},{20,16},{24,28},{28,24},{1,5},{5... | collective-permute-start | bytes 417800 | tf_op jit(solution)/shard_map/ppermute | solution.py:720
  12.7 16.8 %collective-permute-start.5 = (bf16[2,4,64,512]{3,2,1,0:T(8,128)(2,1)S(1)}, bf16[2,4,64,512]{3,2,1,0:T(8,128)(2,1)S(1)}, u32[]{:S(2)}, u32[]{:S(2)}) collective-permute-start(bf16[2,4,64,512]{3,2,1,0:T(8,128)(2,1)S(1)} %pad_maximum_fusion.refs_0_), channel_id=1, source_target_pairs={{0,8},{4,12},{8,16},{12,20},{16,24},{20,28},{24,0},{28,4},{1,9},{5... | collective-permute-start | bytes 1572872 | tf_op jit(solution)/shard_map/ppermute | solution.py:717
  14.3 15.2 %collective-permute-start.6 = (bf16[2,4,64,512]{3,2,1,0:T(8,128)(2,1)S(1)}, bf16[2,4,64,512]{3,2,1,0:T(8,128)(2,1)S(1)}, u32[]{:S(2)}, u32[]{:S(2)}) collective-permute-start(bf16[2,4,64,512]{3,2,1,0:T(8,128)(2,1)S(1)} %pad_maximum_fusion.refs_0_), channel_id=1, source_target_pairs={{0,4},{4,0},{8,12},{12,8},{16,20},{20,16},{24,28},{28,24},{1,5},{5... | collective-permute-start | bytes 1572872 | tf_op jit(solution)/shard_map/ppermute | solution.py:720
  18.4 11.1 %collective-permute-start.4 = (bf16[2,272,128]{2,1,0:T(8,128)(2,1)S(1)}, bf16[2,272,128]{2,1,0:T(8,128)(2,1)S(1)}, u32[]{:S(2)}, u32[]{:S(2)}) collective-permute-start(bf16[2,272,128]{2,1,0:T(8,128)(2,1)S(1)} %collective-permute-done.2.refs_2_), channel_id=1, source_target_pairs={{0,8},{4,12},{8,16},{12,20},{16,24},{20,28},{24,0},{28,4},{1,9},{5... | collective-permute-start | bytes 417800 | tf_op jit(solution)/shard_map/ppermute | solution.py:717
  20.0 9.1 %collective-permute-start.3 = (bf16[2,272,128]{2,1,0:T(8,128)(2,1)S(1)}, bf16[2,272,128]{2,1,0:T(8,128)(2,1)S(1)}, u32[]{:S(2)}, u32[]{:S(2)}) collective-permute-start(bf16[2,272,128]{2,1,0:T(8,128)(2,1)S(1)} %collective-permute-done.2.refs_2_), channel_id=1, source_target_pairs={{0,4},{4,0},{8,12},{12,8},{16,20},{20,16},{24,28},{28,24},{1,5},{5... | collective-permute-start | bytes 417800 | tf_op jit(solution)/shard_map/ppermute | solution.py:720
  26.5 13.6 %collective-permute-start.10 = (bf16[416,512]{1,0:T(8,128)(2,1)}, bf16[416,512]{1,0:T(8,128)(2,1)S(1)}, u32[]{:S(2)}, u32[]{:S(2)}) collective-permute-start(bf16[416,512]{1,0:T(8,128)(2,1)} %get-tuple-element.75.dy_own.dy), channel_id=1, source_target_pairs={{0,2},{1,3},{2,0},{3,1},{4,6},{5,7},{6,4},{7,5},{8,10},{9,11},{10,... | collective-permute-start | bytes 1277960 | tf_op jit(solution)/shard_map/ppermute | solution.py:669
  30.9 6.9 %collective-permute-start.8 = (bf16[2,272,128]{2,1,0:T(8,128)(2,1)S(1)}, bf16[2,272,128]{2,1,0:T(8,128)(2,1)S(1)}, u32[]{:S(2)}, u32[]{:S(2)}) collective-permute-start(bf16[2,272,128]{2,1,0:T(8,128)(2,1)S(1)} %collective-permute-done.4.refs_4_), channel_id=1, source_target_pairs={{0,8},{4,12},{8,16},{12,20},{16,24},{20,28},{24,0},{28,4},{1,9},{5... | collective-permute-start | bytes 417800 | tf_op jit(solution)/shard_map/ppermute | solution.py:717
  47.4 16.2 %collective-permute-start.18 = (bf16[2,4,64,512]{3,2,1,0:T(8,128)(2,1)S(1)}, bf16[2,4,64,512]{3,2,1,0:T(8,128)(2,1)S(1)}, u32[]{:S(2)}, u32[]{:S(2)}) collective-permute-start(bf16[2,4,64,512]{3,2,1,0:T(8,128)(2,1)S(1)} %collective-permute-done.5.refs_2_), channel_id=1, source_target_pairs={{0,8},{4,12},{8,16},{12,20},{16,24},{20,28},{24,0},{28,4},{1,9},{5... | collective-permute-start | bytes 1572872 | tf_op jit(solution)/shard_map/ppermute | solution.py:717
  47.5 15.5 %collective-permute-start.19 = (bf16[2,4,64,512]{3,2,1,0:T(8,128)(2,1)S(1)}, bf16[2,4,64,512]{3,2,1,0:T(8,128)(2,1)}, u32[]{:S(2)}, u32[]{:S(2)}) collective-permute-start(bf16[2,4,64,512]{3,2,1,0:T(8,128)(2,1)S(1)} %collective-permute-done.5.refs_2_), channel_id=1, source_target_pairs={{0,4},{4,0},{8,12},{12,8},{16,20},{20,16},{24,28},{28,24},{1,5},{5... | collective-permute-start | bytes 1572872 | tf_op jit(solution)/shard_map/ppermute | solution.py:720
  48.9 24.2 %collective-permute-start.13 = (bf16[2,4,64,512]{3,2,1,0:T(8,128)(2,1)S(1)}, bf16[2,4,64,512]{3,2,1,0:T(8,128)(2,1)S(1)}, u32[]{:S(2)}, u32[]{:S(2)}) collective-permute-start(bf16[2,4,64,512]{3,2,1,0:T(8,128)(2,1)S(1)} %pad_maximum_fusion.1.refs_0_), channel_id=1, source_target_pairs={{0,4},{4,0},{8,12},{12,8},{16,20},{20,16},{24,28},{28,24},{1,5},{5... | collective-permute-start | bytes 1572872 | tf_op jit(solution)/shard_map/ppermute | solution.py:720
  61.3 12.2 %collective-permute-start.15 = (bf16[416,512]{1,0:T(8,128)(2,1)}, bf16[416,512]{1,0:T(8,128)(2,1)}, u32[]{:S(2)}, u32[]{:S(2)}) collective-permute-start(bf16[416,512]{1,0:T(8,128)(2,1)} %get-tuple-element.84.own), channel_id=1, source_target_pairs={{0,2},{1,3},{2,0},{3,1},{4,6},{5,7},{6,4},{7,5},{8,10},{9,11},{10,... | collective-permute-start | bytes 1277960 | tf_op jit(solution)/shard_map/ppermute | solution.py:669
  62.9 15.5 %collective-permute-start.14 = (bf16[2,4,64,512]{3,2,1,0:T(8,128)(2,1)S(1)}, bf16[2,4,64,512]{3,2,1,0:T(8,128)(2,1)S(1)}, u32[]{:S(2)}, u32[]{:S(2)}) collective-permute-start(bf16[2,4,64,512]{3,2,1,0:T(8,128)(2,1)S(1)} %pad_maximum_fusion.1.refs_0_), channel_id=1, source_target_pairs={{0,8},{4,12},{8,16},{12,20},{16,24},{20,28},{24,0},{28,4},{1,9},{5... | collective-permute-start | bytes 1572872 | tf_op jit(solution)/shard_map/ppermute | solution.py:717
  63.0 15.4 %collective-permute-start.22 = (bf16[416,512]{1,0:T(8,128)(2,1)S(1)}, bf16[416,512]{1,0:T(8,128)(2,1)S(1)}, u32[]{:S(2)}, u32[]{:S(2)}) collective-permute-start(bf16[416,512]{1,0:T(8,128)(2,1)S(1)} %copy-done.32), channel_id=1, source_target_pairs={{0,1},{1,0},{2,3},{3,2},{4,5},{5,4},{6,7},{7,6},{8,9},{9,8},{10,11... | collective-permute-start | bytes 1277960 | tf_op jit(solution)/shard_map/ppermute | solution.py:669
  63.6 16.2 %collective-permute-start.23 = (bf16[416,512]{1,0:T(8,128)(2,1)}, bf16[416,512]{1,0:T(8,128)(2,1)S(1)}, u32[]{:S(2)}, u32[]{:S(2)}) collective-permute-start(bf16[416,512]{1,0:T(8,128)(2,1)} %copy-done.33), channel_id=1, source_target_pairs={{0,1},{1,0},{2,3},{3,2},{4,5},{5,4},{6,7},{7,6},{8,9},{9,8},{10,11... | collective-permute-start | bytes 1277960 | tf_op jit(solution)/shard_map/ppermute | solution.py:669
  73.6 7.0 %collective-permute-start.21 = (bf16[416,512]{1,0:T(8,128)(2,1)}, bf16[416,512]{1,0:T(8,128)(2,1)S(1)}, u32[]{:S(2)}, u32[]{:S(2)}) collective-permute-start(bf16[416,512]{1,0:T(8,128)(2,1)} %collective-permute-done.15.side), channel_id=1, source_target_pairs={{0,1},{1,0},{2,3},{3,2},{4,5},{5,4},{6,7},{7,6},{8,9},{9,8},{10,11... | collective-permute-start | bytes 1277960 | tf_op jit(solution)/shard_map/ppermute | solution.py:669
  78.4 20.2 %collective-permute-start.24 = (bf16[2,4,64,512]{3,2,1,0:T(8,128)(2,1)S(1)}, bf16[2,4,64,512]{3,2,1,0:T(8,128)(2,1)S(1)}, u32[]{:S(2)}, u32[]{:S(2)}) collective-permute-start(bf16[2,4,64,512]{3,2,1,0:T(8,128)(2,1)S(1)} %collective-permute-done.18.refs_4_), channel_id=1, source_target_pairs={{0,8},{4,12},{8,16},{12,20},{16,24},{20,28},{24,0},{28,4},{1,9},{5... | collective-permute-start | bytes 1572872 | tf_op jit(solution)/shard_map/ppermute | solution.py:717
  78.4 20.1 %collective-permute-start.26 = (bf16[2,4,64,512]{3,2,1,0:T(8,128)(2,1)S(1)}, bf16[2,4,64,512]{3,2,1,0:T(8,128)(2,1)S(1)}, u32[]{:S(2)}, u32[]{:S(2)}) collective-permute-start(bf16[2,4,64,512]{3,2,1,0:T(8,128)(2,1)S(1)} %collective-permute-done.18.refs_4_), channel_id=1, source_target_pairs={{0,4},{4,0},{8,12},{12,8},{16,20},{20,16},{24,28},{28,24},{1,5},{5... | collective-permute-start | bytes 1572872 | tf_op jit(solution)/shard_map/ppermute | solution.py:720
  79.9 26.4 %collective-permute-start.17 = (bf16[2,4,64,512]{3,2,1,0:T(8,128)(2,1)S(1)}, bf16[2,4,64,512]{3,2,1,0:T(8,128)(2,1)S(1)}, u32[]{:S(2)}, u32[]{:S(2)}) collective-permute-start(bf16[2,4,64,512]{3,2,1,0:T(8,128)(2,1)S(1)} %collective-permute-done.14.refs_2_), channel_id=1, source_target_pairs={{0,8},{4,12},{8,16},{12,20},{16,24},{20,28},{24,0},{28,4},{1,9},{5... | collective-permute-start | bytes 1572872 | tf_op jit(solution)/shard_map/ppermute | solution.py:717
  79.9 24.2 %collective-permute-start.16 = (bf16[2,4,64,512]{3,2,1,0:T(8,128)(2,1)S(1)}, bf16[2,4,64,512]{3,2,1,0:T(8,128)(2,1)S(1)}, u32[]{:S(2)}, u32[]{:S(2)}) collective-permute-start(bf16[2,4,64,512]{3,2,1,0:T(8,128)(2,1)S(1)} %collective-permute-done.14.refs_2_), channel_id=1, source_target_pairs={{0,4},{4,0},{8,12},{12,8},{16,20},{20,16},{24,28},{28,24},{1,5},{5... | collective-permute-start | bytes 1572872 | tf_op jit(solution)/shard_map/ppermute | solution.py:720
  98.7 13.3 %collective-permute-start.27 = (bf16[2,2,64,512]{3,2,1,0:T(8,128)(2,1)S(1)}, bf16[2,2,64,512]{3,2,1,0:T(8,128)(2,1)S(1)}, u32[]{:S(2)}, u32[]{:S(2)}) collective-permute-start(bf16[2,2,64,512]{3,2,1,0:T(8,128)(2,1)S(1)} %slice.53), channel_id=1, source_target_pairs={{0,8},{4,12},{8,16},{12,20},{16,24},{20,28},{24,0},{28,4},{1,9},{5... | collective-permute-start | bytes 786440 | tf_op jit(solution)/shard_map/ppermute | solution.py:717
  100.1 11.8 %collective-permute-start.25 = (bf16[2,2,64,512]{3,2,1,0:T(8,128)(2,1)S(1)}, bf16[2,2,64,512]{3,2,1,0:T(8,128)(2,1)S(1)}, u32[]{:S(2)}, u32[]{:S(2)}) collective-permute-start(bf16[2,2,64,512]{3,2,1,0:T(8,128)(2,1)S(1)} %slice.52), channel_id=1, source_target_pairs={{0,4},{4,0},{8,12},{12,8},{16,20},{20,16},{24,28},{28,24},{1,5},{5... | collective-permute-start | bytes 786440 | tf_op jit(solution)/shard_map/ppermute | solution.py:720
  106.3 24.2 %collective-permute-start.29 = (bf16[2,4,64,512]{3,2,1,0:T(8,128)(2,1)S(1)}, bf16[2,4,64,512]{3,2,1,0:T(8,128)(2,1)S(1)}, u32[]{:S(2)}, u32[]{:S(2)}) collective-permute-start(bf16[2,4,64,512]{3,2,1,0:T(8,128)(2,1)S(1)} %collective-permute-done.17.refs_4_), channel_id=1, source_target_pairs={{0,8},{4,12},{8,16},{12,20},{16,24},{20,28},{24,0},{28,4},{1,9},{5... | collective-permute-start | bytes 1572872 | tf_op jit(solution)/shard_map/ppermute | solution.py:717
  111.9 19.4 %collective-permute-start.28 = (bf16[2,4,64,512]{3,2,1,0:T(8,128)(2,1)S(1)}, bf16[2,4,64,512]{3,2,1,0:T(8,128)(2,1)S(1)}, u32[]{:S(2)}, u32[]{:S(2)}) collective-permute-start(bf16[2,4,64,512]{3,2,1,0:T(8,128)(2,1)S(1)} %collective-permute-done.17.refs_4_), channel_id=1, source_target_pairs={{0,4},{4,0},{8,12},{12,8},{16,20},{20,16},{24,28},{28,24},{1,5},{5... | collective-permute-start | bytes 1572872 | tf_op jit(solution)/shard_map/ppermute | solution.py:720
  131.4 8.4 %collective-permute-start.31 = (bf16[2,2,64,512]{3,2,1,0:T(8,128)(2,1)S(1)}, bf16[2,2,64,512]{3,2,1,0:T(8,128)(2,1)S(1)}, u32[]{:S(2)}, u32[]{:S(2)}) collective-permute-start(bf16[2,2,64,512]{3,2,1,0:T(8,128)(2,1)S(1)} %slice.55), channel_id=1, source_target_pairs={{0,8},{4,12},{8,16},{12,20},{16,24},{20,28},{24,0},{28,4},{1,9},{5... | collective-permute-start | bytes 786440 | tf_op jit(solution)/shard_map/ppermute | solution.py:717
  176.8 11.9 %collective-permute-start.33 = (bf16[416,512]{1,0:T(8,128)(2,1)S(1)}, bf16[416,512]{1,0:T(8,128)(2,1)S(1)}, u32[]{:S(2)}, u32[]{:S(2)}) collective-permute-start(bf16[416,512]{1,0:T(8,128)(2,1)S(1)} %fusion), channel_id=1, source_target_pairs={{0,2},{1,3},{2,0},{3,1},{4,6},{5,7},{6,4},{7,5},{8,10},{9,11},{10,... | collective-permute-start | bytes 1277960 | tf_op jit(solution)/shard_map/ppermute | solution.py:669
  177.3 23.9 %all-to-all-start.1 = ((bf16[8,96,512]{2,1,0:T(8,128)(2,1)}), bf16[8,96,512]{2,1,0:T(8,128)(2,1)S(1)}, u32[]{:S(2)}, u32[]{:S(2)}) async-start(bf16[8,96,512]{2,1,0:T(8,128)(2,1)} %get-tuple-element.120), calls=%async_computation.1 | async-start | bytes 1572864 | tf_op jit(solution)/shard_map/all_to_all | solution.py:960
  201.3 14.2 %all-to-all-start = ((bf16[32,32,128]{2,1,0:T(8,128)(2,1)}), bf16[32,32,128]{2,1,0:T(8,128)(2,1)S(1)}, u32[]{:S(2)}, u32[]{:S(2)}) async-start(bf16[32,32,128]{2,1,0:T(8,128)(2,1)} %get-tuple-element.110), calls=%async_computation | async-start | bytes 524288 | tf_op jit(solution)/shard_map/all_to_all | solution.py:981
  204.9 17.0 %collective-permute-start.34 = (bf16[2,416,512]{2,1,0:T(8,128)(2,1)}, bf16[2,416,512]{2,1,0:T(8,128)(2,1)S(1)}, u32[]{:S(2)}, u32[]{:S(2)}) collective-permute-start(bf16[2,416,512]{2,1,0:T(8,128)(2,1)} %get-tuple-element.114), channel_id=1, source_target_pairs={{0,1},{1,0},{2,3},{3,2},{4,5},{5,4},{6,7},{7,6},{8,9},{9,8},{10,11... | collective-permute-start | bytes 2555912 | tf_op jit(solution)/shard_map/ppermute | solution.py:669
  218.4 21.1 %all-to-all-start.2 = ((bf16[8,80,512]{2,1,0:T(8,128)(2,1)}), bf16[8,80,512]{2,1,0:T(8,128)(2,1)S(1)}, u32[]{:S(2)}, u32[]{:S(2)}) async-start(bf16[8,80,512]{2,1,0:T(8,128)(2,1)} %shard_map.268), calls=%async_computation.2 | async-start | bytes 1310720 | tf_op jit(solution)/shard_map/all_to_all | solution.py:1005
  222.1 11.7 %collective-permute-start.35 = (bf16[416,512]{1,0:T(8,128)(2,1)S(1)}, bf16[416,512]{1,0:T(8,128)(2,1)S(1)}, u32[]{:S(2)}, u32[]{:S(2)}) collective-permute-start(bf16[416,512]{1,0:T(8,128)(2,1)S(1)} %fusion.1), channel_id=1, source_target_pairs={{0,2},{1,3},{2,0},{3,1},{4,6},{5,7},{6,4},{7,5},{8,10},{9,11},{10,... | collective-permute-start | bytes 1277960 | tf_op jit(solution)/shard_map/ppermute | solution.py:669
  239.6 7.0 %collective-permute-start.39 = (bf16[256,512]{1,0:T(8,128)(2,1)S(1)}, bf16[256,512]{1,0:T(8,128)(2,1)S(1)}, u32[]{:S(2)}, u32[]{:S(2)}) collective-permute-start(bf16[256,512]{1,0:T(8,128)(2,1)S(1)} %pad_maximum_fusion.2.own), channel_id=1, source_target_pairs={{0,2},{1,3},{2,0},{3,1},{4,6},{5,7},{6,4},{7,5},{8,10},{9,11},{10,... | collective-permute-start | bytes 786440 | tf_op jit(solution)/shard_map/ppermute | solution.py:669
  (68 other events, 650.1 us)
where the time goes:
time: 254 us; the launch traced here: 253 us
  Pallas kernels  111 us (44%)
  waiting for transfers between devices  75.6 us (30%)
  starting transfers between devices  46 us (18%)
  local copies, waits for them, and re-layouts  15.9 us (6%)
  other arithmetic  3.92 us (2%)
    pallas_call x3, Pallas kernels, build(): return call(body, outs, scratch, 0, (), specs, None, cost, vmem)(*args)  38.4 us
    ppermute x18, waiting for transfers between devices, swap(): return lax.ppermute(value, 'tensor', [(at, at ^ bit) for at in range(size)])  33.2 us
    pallas_call x1, Pallas kernels, per_device(): call(partial(late_kernel, size, base), (half, half, half, half, like((8,...  32.2 us
    ppermute x12, waiting for transfers between devices, across(): return lax.ppermute(value, 'dp', [(at, at ^ 1) for at in range(self.size)])  19.6 us
    ppermute x11, waiting for transfers between devices, along(): lax.ppermute(value, 'dp', [(at, (at + 2) % size) for at in range(size)])  18.1 us
    pallas_call x1, Pallas kernels, per_device(): call(partial(early_kernel, size, base), (like((base, expert_slots, row_wi...  17.1 us
    ppermute x12, starting transfers between devices, across(): return lax.ppermute(value, 'dp', [(at, at ^ 1) for at in range(self.size)])  13.4 us
    ppermute x18, starting transfers between devices, swap(): return lax.ppermute(value, 'tensor', [(at, at ^ bit) for at in range(size)])  13 us
  transfers between devices with their start and end apart: 44, of which 26 were waited for; matrix products, arithmetic and copies ran while one was open for 3% of the time, Pallas kernels for 29%

commit v1 on v0

--- a/solution.py
+++ b/solution.py
@@ -77,15 +77,19 @@
     options = {}
     if grid is not None:
         options = dict(grid=grid, in_specs=in_specs, out_specs=out_specs)
+    elif in_specs is not None:
+        options = dict(in_specs=in_specs, out_specs=out_specs)
     elif smem:
         def build(*args):
             specs = [pl.BlockSpec(memory_space=pltpu.SMEM)] * smem
             specs += [pl.BlockSpec(memory_space=pltpu.VMEM)] * (len(args) - smem)
-            return call(body, outs, scratch, 0, (), specs, None, cost, vmem)(*args)
+            if isinstance(outs, tuple):
+                ends = (pl.BlockSpec(memory_space=pltpu.VMEM),) * len(outs)
+            else:
+                ends = pl.BlockSpec(memory_space=pltpu.VMEM)
+            return call(body, outs, scratch, 0, None, specs, ends, cost, vmem)(*args)
 
         return build
-    if grid == ():
-        options = dict(in_specs=in_specs)
     return pl.pallas_call(
         body,
         out_shape=outs,
@@ -243,16 +247,29 @@
     start = table[expert, 4 + chunk]
     target = table[expert, 8 + chunk]
 
-    def move(unit, carry):
-        here = pl.ds(pl.multiple_of((start + unit) * UNIT, UNIT), UNIT)
-        there = pl.ds(pl.multiple_of((target + unit) * UNIT, UNIT), UNIT)
+    count = table[expert, chunk]
+
+    def move(unit, units):
+        here = pl.ds(pl.multiple_of((start + unit) * UNIT, UNIT), units * UNIT)
+        there = pl.ds(pl.multiple_of((target + unit) * UNIT, UNIT), units * UNIT)
         if forward:
             expert_ref[there, :] = chunk_ref[here, :]
         else:
             chunk_ref[here, :] = expert_ref[there, :]
+
+    def four(step, carry):
+        move(4 * step, 4)
         return carry
 
-    lax.fori_loop(0, table[expert, chunk], move, 0)
+    lax.fori_loop(0, lax.shift_right_logical(count, 2), four, 0)
+
+    @pl.when(lax.bitwise_and(count, 2) != 0)
+    def _():
+        move(count - lax.bitwise_and(count, 3), 2)
+
+    @pl.when(lax.bitwise_and(count, 1) != 0)
+    def _():
+        move(count - 1, 1)
 
 
 def clear_units(ref, start):
@@ -317,7 +334,9 @@
     lax.fori_loop(0, EXPERTS, clear, 0)
 
 
-def expert_body(expert, slots, w_in, w_out, up_hid, down_hid, up_exo, down, g_hid, g_exo, out):
+def expert_body(
+    expert, slots, w_in, w_out, up_hid, down_hid, up_exo, down, g_hid, g_exo, grad_out, mix_out
+):
     width = w_in.shape[0]
     lane = lanes((1, 128))
     x = slots[:, 0:width]
@@ -346,13 +365,14 @@
     g_exo[1] += tdot(ocode, back)
     high = gate_grad.astype(BF16).astype(F32)
     spread = jnp.where(here, jnp.where(lane < EXPERTS, high, gate_grad - high), 0.0)
-    out[:, 0:width] = (gate * returned).astype(BF16)
-    out[:, width : 2 * width] = x_grad.astype(BF16)
-    out[:, 2 * width : 2 * width + 128] = spread.astype(BF16)
-
-
-def fetch_weights(parts, joined, sems, step, count):
-    owners = block_owners(min(len(parts), 8))
+    mix_out[...] = (gate * returned).astype(BF16)
+    grad_out[:, 0:width] = x_grad.astype(BF16)
+    grad_out[:, width : width + 128] = spread.astype(BF16)
+
+
+def fetch_weights(parts, pieces, joined, sems, step, count, first):
+    common = len(parts) - len(pieces)
+    owners = block_owners(common + 1 if pieces else common)
     feats = parts[0].shape[2]
     slot = lax.rem(step, 2)
 
@@ -363,29 +383,21 @@
         )
 
     def start(expert, slot):
-        for place in range(len(owners) - 1):
+        for place in range(common):
             copies(parts[place], expert, slot, place).start()
-        place = len(owners) - 1
-        if len(parts) == len(owners):
-            copies(parts[place], expert, slot, place).start()
-            return
-        half = parts[place].shape[1]
-
-        @pl.when(expert < half)
-        def _():
-            copies(parts[place], expert, slot, place).start()
-
-        @pl.when(expert >= half)
-        def _():
-            copies(parts[place + 1], expert - half, slot, place).start()
+        for part, begin in zip(parts[common:], pieces):
+
+            @pl.when(jnp.logical_and(expert >= begin, expert < begin + part.shape[1]))
+            def _():
+                copies(part, expert - begin, slot, common).start()
 
     @pl.when(step == 0)
     def _():
-        start(0, 0)
+        start(step + first, 0)
 
     @pl.when(step + 1 < count)
     def _():
-        start(step + 1, 1 - slot)
+        start(step + 1 + first, 1 - slot)
 
     for place in range(len(owners)):
         copies(parts[place], 0, slot, place).wait()
@@ -403,86 +415,108 @@
     return owners
 
 
-def early_kernel(size, count, *refs):
+def expert_kernel(size, pieces, count, first, base, *refs):
     parts, refs = refs[:size], refs[size:]
-    slots, up_hid, down_hid, up_exo, down, out, g_hid, g_exo, joined, sems = refs
+    slots, up_hid, down_hid, up_exo, down, *before, grad_out, mix_out = refs[:-4]
+    g_hid, g_exo, joined, sems = refs[-4:]
     step = pl.program_id(0)
 
     @pl.when(step == 0)
     def _():
-        g_hid[...] = jnp.zeros_like(g_hid)
-        g_exo[...] = jnp.zeros_like(g_exo)
-
-    w_in, w_out = fetch_weights(parts, joined, sems, step, count)
+        g_hid[...] = before[0][...] if before else jnp.zeros_like(g_hid)
+        g_exo[...] = before[1][...] if before else jnp.zeros_like(g_exo)
+
+    w_in, w_out = fetch_weights(parts, pieces, joined, sems, step, count, first)
     expert_body(
-        step, slots.at[0], w_in, w_out, up_hid, down_hid, up_exo, down,
-        g_hid, g_exo, out.at[0],
-    )
-
-
-def late_kernel(size, base, *refs):
+        step + base, slots.at[0], w_in, w_out, up_hid, down_hid, up_exo, down,
+        g_hid, g_exo, grad_out.at[0], mix_out.at[0],
+    )
+
+
+def collect_chunk(table, chunk, sources, packed):
+    base = 0
+    for source in sources:
+
+        def collect(expert, carry, source=source, base=base):
+            move_units(table, chunk, expert + base, packed, source.at[expert], False)
+            return carry
+
+        lax.fori_loop(0, source.shape[0], collect, 0)
+        base += source.shape[0]
+    ending = EXPERTS - 1
+    clear_units(packed, table[ending, 4 + chunk] + table[ending, chunk])
+
+
+def chosen_slots(place, chunk, packed):
+    shape = (place.shape[1], packed.shape[0])
+    spot = lanes(shape).astype(F32)
+    chosen = jnp.logical_or(spot == place[chunk, :, 0:1], spot == place[chunk, :, 1:2])
+    return jnp.where(chosen, 1.0, 0.0).astype(BF16)
+
+
+def last_kernel(size, pieces, count, first, base, *refs):
     parts, refs = refs[:size], refs[size:]
     (
-        slots, up_hid, down_hid, up_exo, down, before, g_hid_before, g_exo_before,
-        adapter, table, normed, rcode, prob, place, router, up_router,
-        mix_keep, mix_send, grad_keep, grad_send, grads_out,
-        joined, sems, late, g_hid, g_exo, g_router, packed,
-    ) = refs
+        slots, up_hid, down_hid, up_exo, down, g_hid_before, g_exo_before,
+        adapter, table, place, router, up_router, *waiting,
+    ) = refs[:-15]
+    (
+        mix_out, grad_keep, grad_send, grads_out,
+        joined, sems, collected, g_hid, g_exo, g_router, packed, normed, rcode, prob, came,
+    ) = refs[-15:]
     step = pl.program_id(0)
     width = down.shape[2]
     lane = lanes((1, 128))
+    targets, at = [], 0
+    for source in waiting[:-3]:
+        targets.append(collected.at[at : at + source.shape[0]])
+        at += source.shape[0]
+    targets += [normed, rcode, prob]
+    arrivals = [
+        pltpu.make_async_copy(source, target, came.at[index])
+        for index, (source, target) in enumerate(zip(waiting, targets))
+    ]
 
     @pl.when(step == 0)
     def _():
         g_hid[...] = g_hid_before[...]
         g_exo[...] = g_exo_before[...]
         g_router[...] = jnp.zeros_like(g_router)
-
-    w_in, w_out = fetch_weights(parts, joined, sems, step, EXPERTS - base)
+        for arrival in arrivals:
+            arrival.start()
+
+    w_in, w_out = fetch_weights(parts, pieces, joined, sems, step, count, first)
     expert_body(
         step + base, slots.at[0], w_in, w_out, up_hid, down_hid, up_exo, down,
-        g_hid, g_exo, late.at[step],
-    )
-
-    @pl.when(step == pl.num_programs(0) - 1)
+        g_hid, g_exo, collected.at[step + base], mix_out.at[0],
+    )
+
+    @pl.when(step == count - 1)
     def _():
         me = lax.axis_index("tensor")
-        count = mix_keep.shape[1]
-
-        def combine(index, mix_out, grad_out):
+        tall = normed.shape[1]
+        for arrival in arrivals:
+            arrival.wait()
+
+        def combine(index, grad_out):
             chunk = lax.bitwise_xor(me, index)
-            for base_expert, source in ((0, before), (base, late)):
-
-                def collect(expert, carry):
-                    move_units(
-                        table, chunk, expert + base_expert, packed, source.at[expert], False
-                    )
-                    return carry
-
-                lax.fori_loop(0, source.shape[0], collect, 0)
-            ending = EXPERTS - 1
-            clear_units(packed, table[ending, 4 + chunk] + table[ending, chunk])
-            spot = lanes((count, packed.shape[0])).astype(F32)
-            chosen = jnp.logical_or(
-                spot == place[chunk, :, 0:1], spot == place[chunk, :, 1:2]
-            )
-            total = dot(jnp.where(chosen, 1.0, 0.0).astype(BF16), packed[...])
-            mask = jnp.where(lane // RANK == row_adapters(adapter, chunk, count), 1.0, 0.0)
-            mix_out[...] = total[:, 0:width].astype(BF16)
-            gates = total[:, 2 * width : 2 * width + 128]
+            collect_chunk(table, chunk, [collected], packed)
+            total = dot(chosen_slots(place, chunk, packed), packed[...])
+            mask = jnp.where(lane // RANK == row_adapters(adapter, chunk, tall), 1.0, 0.0)
+            gates = total[:, width : width + 128]
             probs = jnp.where(lane < 2 * EXPERTS, prob[index], 0.0)
             mean = jnp.sum(probs * gates, -1, keepdims=True)
             logit = (probs * (gates - jnp.where(lane < EXPERTS, mean, 0.0))).astype(BF16)
             rcode_grad = (mask * dot(logit, up_router[...])).astype(BF16)
-            grad = total[:, width : 2 * width] + dot(logit, router[...])
+            grad = total[:, 0:width] + dot(logit, router[...])
             grad = grad + dot(rcode_grad, down[4])
             grad_out[...] = grad.astype(BF16)
             g_router[0] += tdot(rcode_grad, normed[index])
             g_router[1, :, 0:128] += tdot(logit, rcode[index])
 
         def pair(half, carry):
-            combine(2 * half, mix_keep.at[half], grad_keep.at[half])
-            combine(2 * half + 1, mix_send.at[half], grad_send.at[half])
+            combine(2 * half, grad_keep.at[half])
+            combine(2 * half + 1, grad_send.at[half])
             return carry
 
         lax.fori_loop(0, 2, pair, 0)
@@ -497,6 +531,23 @@
             grads_out[owner, 0:64, :] = shared[member][at : at + 64, :].astype(BF16)
             member, at = divmod(owner * 32, CODE)
             grads_out[owner, 64:96, :] = g_hid[member, at : at + 32, :].astype(BF16)
+
+
+def mix_kernel(table, place, *refs):
+    sources, (mix_keep, mix_send, packed) = refs[:-3], refs[-3:]
+    me = lax.axis_index("tensor")
+
+    def combine(index, mix_out):
+        chunk = lax.bitwise_xor(me, index)
+        collect_chunk(table, chunk, sources, packed)
+        mix_out[...] = dot(chosen_slots(place, chunk, packed), packed[...]).astype(BF16)
+
+    def pair(half, carry):
+        combine(2 * half, mix_keep.at[half])
+        combine(2 * half + 1, mix_send.at[half])
+        return carry
+
+    lax.fori_loop(0, 2, pair, 0)
 
 
 def backward_kernel(
@@ -634,7 +685,9 @@
             early[owner // 2][rows, :] = part[
                 128 + owner * 16 : 144 + owner * 16, :
             ].astype(F32)
-    router_out[...] = router[0:EXPERTS, 0:CODE] + router[EXPERTS : 2 * EXPERTS, 0:CODE]
+    total = router[0:EXPERTS, 0:CODE] + router[EXPERTS : 2 * EXPERTS, 0:CODE]
+    for adapter in range(ADAPTERS):
+        router_out[adapter] = total[:, adapter * RANK : (adapter + 1) * RANK]
 
 
 def input_kernel(
@@ -682,7 +735,7 @@
 def reduce_pair(keep, send):
     came = swap(send, 1)
     other = (keep[1].astype(F32) + came[1].astype(F32)).astype(BF16)
-    return keep, came, swap(other, 2)
+    return (keep, came, swap(other, 2)), other
 
 
 def gather_projections(shards, extra, ids, others):
@@ -729,9 +782,12 @@
         if split is None:
             block = after(self.block, *self.done, *waits)
             return self.parts + [block, self.across(block)]
-        passed, crossed = (after(value, *waits) for value in self.done)
-        halves = self.across(passed[:, :split]), self.along(crossed[:, split:])
-        return self.parts + [passed, *halves]
+        passed, crossed = self.done
+        return (
+            self.parts + [passed],
+            self.across(after(passed, *waits[:1])[:, :split]),
+            lambda *waits: self.along(after(crossed, *waits)[:, split:]),
+        )
 
 
 class Whole:
@@ -743,7 +799,7 @@
         pass
 
     def finish(self, *waits, split=None):
-        return self.parts
+        return self.parts, None, lambda *waits: None
 
 
 def per_device(
@@ -875,91 +931,108 @@
         cost=cost(17),
     )(adapter_index, table, *normed2_four, *dy_four, place, down, router, router_up)
 
-    early_parts = early_ring.finish(slots, split=base // 2)
+    part = base // 2
+    common, near, far = early_ring.finish(slots, split=part)
+    far = far(slots)
     ready = late_ring.done
-    late_ring.step(slots, across=early_parts[7:])
+    late_ring.step(slots, across=(near, far) if fits else ())
     whole = lambda *shape: pl.BlockSpec(shape, lambda step: (0,) * len(shape))
     smem = pl.BlockSpec(memory_space=pltpu.SMEM)
-    size = len(early_parts)
-    shard = pl.BlockSpec(memory_space=pltpu.HBM)
+    vmem = pl.BlockSpec(memory_space=pltpu.VMEM)
+    hbm = pl.BlockSpec(memory_space=pltpu.HBM)
     joined = [
         pltpu.VMEM((2, 2, width, hidden), BF16),
-        pltpu.SemaphoreType.DMA((2, min(size, 8))),
+        pltpu.SemaphoreType.DMA((2, 8 if fits else 1)),
     ]
+    each = lambda wide, first: pl.BlockSpec(
+        (1, expert_slots, wide), lambda step: (step + first, 0, 0)
+    )
     small = [
         whole(CODE, hidden), whole(CODE, hidden), whole(CODE, width), whole(5, CODE, width),
     ]
-    early_out, g_hid, g_exo = call(
-        partial(early_kernel, size, base),
-        (
-            like((base, expert_slots, row_wide), BF16),
-            like((2, CODE, hidden), F32),
-            like((2, CODE, width), F32),
-        ),
-        scratch=joined,
-        grid=(base,),
-        in_specs=[shard] * size
-        + [pl.BlockSpec((1, expert_slots, row_wide), lambda step: (step, 0, 0))]
-        + small,
-        out_specs=(
-            pl.BlockSpec((1, expert_slots, row_wide), lambda step: (step, 0, 0)),
-            whole(2, CODE, hidden),
-            whole(2, CODE, width),
-        ),
-        cost=cost(16),
-    )(*early_parts, after(slots, *ready), up_hid, down_hid, up_exo, down)
-    late_parts = late_ring.finish(early_out, split=base // 2)
+    sums = [whole(2, CODE, hidden), whole(2, CODE, width)]
+    grad_wide = width + 128
+
+    def experts(parts, pieces, count, first, at, slots, before=()):
+        return call(
+            partial(expert_kernel, len(parts), pieces, count, first, at),
+            (
+                like((count, expert_slots, grad_wide), BF16),
+                like((count, expert_slots, width), BF16),
+                like((2, CODE, hidden), F32),
+                like((2, CODE, width), F32),
+            ),
+            scratch=joined,
+            grid=(count,),
+            in_specs=[hbm] * len(parts) + [each(row_wide, at)] + small + sums[: len(before)],
+            out_specs=(each(grad_wide, 0), each(width, 0), *sums),
+            cost=cost(4 * count),
+        )(*parts, slots, up_hid, down_hid, up_exo, down, *before)
+
+    near, pieces = ([near], (0,)) if fits else ([], ())
+    grad_a, mix_a, *before = experts(
+        common + near, pieces, part, 0, 0, after(slots, *ready)
+    )
+    far, pieces = ([far], (part,)) if fits else ([], ())
+    grad_b, mix_b, *before = experts(
+        common + far, pieces, base - part, part, part, after(slots, *late_ring.done), before
+    )
+    common, near, far = late_ring.finish(grad_a, split=part)
+    halves, pieces = ([near, far(grad_a)], (0, part)) if fits else ([], ())
+    count_last = EXPERTS - base
     half = like((2, count, width), BF16)
     compact = dp == 8 and images == 2 and hidden == width == 512
-    (
-        mix_keep, mix_send, grad_keep, grad_send, early,
-    ) = call(
-        partial(late_kernel, size, base),
+    place = place.swapaxes(1, 2)
+    last_parts = common + halves
+    mix_c, grad_keep, grad_send, early = call(
+        partial(last_kernel, len(last_parts), pieces, count_last, 0, base),
         (
-            half, half, half, half,
+            like((count_last, expert_slots, width), BF16),
+            half, half,
             like((8, 96, width), BF16) if compact else like((6, CODE, width), F32),
         ),
         scratch=joined
         + [
-            pltpu.VMEM((EXPERTS - base, expert_slots, row_wide), BF16),
+            pltpu.VMEM((EXPERTS, expert_slots, grad_wide), BF16),
             pltpu.VMEM((2, CODE, hidden), F32),
             pltpu.VMEM((2, CODE, width), F32),
             pltpu.VMEM((2, CODE, width), F32),
-            pltpu.VMEM((chunk_slots, row_wide), BF16),
+            pltpu.VMEM((chunk_slots, grad_wide), BF16),
+            pltpu.VMEM((tensor, count, width), BF16),
+            pltpu.VMEM((tensor, count, CODE), BF16),
+            pltpu.VMEM((tensor, count, 128), F32),
+            pltpu.SemaphoreType.DMA((5,)),
         ],
-        grid=(EXPERTS - base,),
-        in_specs=[shard] * size
-        + [pl.BlockSpec((1, expert_slots, row_wide), lambda step: (step + base, 0, 0))]
+        grid=(count_last,),
+        in_specs=[hbm] * len(last_parts)
+        + [each(row_wide, base)]
         + small
-        + [
-            whole(base, expert_slots, row_wide),
-            whole(2, CODE, hidden),
-            whole(2, CODE, width),
-            smem,
-            smem,
-            whole(tensor, count, width),
-            whole(tensor, count, CODE),
-            whole(tensor, count, 128),
-            whole(tensor, count, 2),
-            whole(128, width),
-            whole(128, CODE),
-        ],
+        + sums
+        + [smem] * 2
+        + [whole(tensor, count, 2), whole(128, width), whole(128, CODE)]
+        + [hbm] * 5,
         out_specs=(
-            whole(2, count, width), whole(2, count, width),
-            whole(2, count, width), whole(2, count, width),
+            each(width, 0), whole(2, count, width), whole(2, count, width),
             whole(8, 96, width) if compact else whole(6, CODE, width),
         ),
-        cost=cost(30),
+        cost=cost(25),
     )(
-        *late_parts, slots, up_hid, down_hid, up_exo, down, early_out, g_hid, g_exo,
-        adapter_index, table, rows, rcode, probs, place.swapaxes(1, 2), router, router_up,
-    )
+        *last_parts, slots, up_hid, down_hid, up_exo, down, *before,
+        adapter_index, table, place, router, router_up, grad_a, grad_b, rows, rcode, probs,
+    )
+    mix_keep, mix_send = call(
+        mix_kernel,
+        (half, half),
+        scratch=[pltpu.VMEM((chunk_slots, width), BF16)],
+        in_specs=[smem] + [vmem] * 4,
+        out_specs=(vmem, vmem),
+        cost=cost(7),
+    )(table, place, mix_a, mix_b, mix_c)
 
     both = ("dp", "tensor")
+    grads, begun = reduce_pair(grad_keep, grad_send)
     if compact:
-        early = lax.all_to_all(early, "dp", 0, 0)
-    grads = reduce_pair(grad_keep, grad_send)
-    mixes = reduce_pair(mix_keep, after(mix_send, grads[2]))
+        early = lax.all_to_all(after(early, begun), "dp", 0, 0)
 
     middle_grad, proj_grad, code_grad, late = call(
         backward_kernel,
@@ -974,11 +1047,12 @@
         cost=cost(11),
         vmem=56,
     )(
-        adapter_index, dy, middle, *grads, norm_gain, weights, up_out,
+        adapter_index, after(dy, mix_send), middle, *grads, norm_gain, weights, up_out,
         normed, code, qkv, prob, mixed, hcode,
     )
     if compact:
         came = lax.all_to_all(late, both, 0, 0)
+    mixes, unused = reduce_pair(mix_keep, after(mix_send, late))
     input_grad = call(
         input_kernel,
         like((local, width), F32),
@@ -998,7 +1072,7 @@
         keep, send, early_hid = call(
             early_sum_kernel, (keep, keep, like((32, width), BF16)), cost=cost(2)
         )(after(early, late))
-        sums = reduce_pair(keep, send)
+        sums, unused = reduce_pair(keep, send)
         packed = call(late_sum_kernel, like((dp, 80, width), BF16), cost=cost(2))(
             came.reshape(dp, CODE, 128), ids, early_hid, *sums
         )
@@ -1014,7 +1088,7 @@
         ) = call(
             unpack_kernel,
             (
-                like((5, CODE, width), F32), whole, whole, like((EXPERTS, CODE), F32),
+                like((5, CODE, width), F32), whole, whole, like((ADAPTERS, EXPERTS, RANK), F32),
                 like((3, CODE, 128), F32), like((CODE, 128), F32), whole, whole,
             ),
             scratch=[pltpu.VMEM((CODE, width), F32)],
@@ -1032,6 +1106,7 @@
         grad_up_out, grad_up_exo = late[7], early_shared[2]
         router_grad = early_shared[3, :, :CODE]
         router_grad = router_grad[:EXPERTS] + router_grad[EXPERTS : 2 * EXPERTS]
+        router_grad = router_grad.reshape(EXPERTS, ADAPTERS, RANK).swapaxes(0, 1)
         grad_up_heads, grad_down_heads = late_heads[:3], late_heads[3]
         grad_up_hidden, grad_down_hidden = early_hid[0], early_hid[1]
     split_up = lambda value: value.reshape(value.shape[:-2] + (ADAPTERS, RANK, value.shape[-1]))
@@ -1039,7 +1114,7 @@
     grad_down_in = split_down(grad_down_in)
     grad_up_out = split_up(grad_up_out)
     grad_up_exo = split_up(grad_up_exo)
-    grad_up_router = router_grad.reshape(EXPERTS, ADAPTERS, RANK).transpose(1, 2, 0)
+    grad_up_router = router_grad.swapaxes(1, 2)
     grad_up_heads = split_up(grad_up_heads)
     grad_down_heads = split_down(grad_down_heads)
     grad_up_hidden = split_up(grad_up_hidden)

time: 254 us -> 250 us (0.984)
  waiting for transfers between devices: 75.6 us -> 60.5 us
  Pallas kernels: 111 us -> 118 us
  starting transfers between devices: 46 us -> 50.3 us
    ppermute x18, waiting for transfers between devices: 33.2 us -> 23.6 us  [swap(): return lax.ppermute(value, 'tensor', [(at, at ^ bit) for at in range(size)])]
    pallas_call x6 -> x8, Pallas kernels: 90.7 us -> 98.5 us  [the longest x3 38 us: build(): return call(body, outs, scratch, 0, None, specs, ends, cost, vmem)(*args)]
    ppermute x12, waiting for transfers between devices: 19.6 us -> 12.9 us  [across(): return lax.ppermute(value, 'dp', [(at, at ^ 1) for at in range(self.size)])]
  transfers between devices with their start and end apart: 44 -> 44, of which waited for: 26 -> 21; matrix products, arithmetic and copies ran while one was open for 3% -> 3% of each run, Pallas kernels for 29% -> 34%
where the time goes in v1:
time: 250 us; the launch traced here: 249 us
  Pallas kernels  118 us (47%)
  waiting for transfers between devices  60.5 us (24%)
  starting transfers between devices  50.3 us (20%)
  local copies, waits for them, and re-layouts  14.6 us (6%)
  other arithmetic  3.92 us (2%)
    pallas_call x3, Pallas kernels, build(): return call(body, outs, scratch, 0, None, specs, ends, cost, vmem)(*args)  38 us
    pallas_call x1, Pallas kernels, per_device(): call(partial(last_kernel, len(last_parts), pieces, count_last, 0, base),...  28.8 us
    ppermute x18, waiting for transfers between devices, swap(): return lax.ppermute(value, 'tensor', [(at, at ^ bit) for at in range(size)])  23.6 us
    pallas_call x2, Pallas kernels, experts(): call(partial(expert_kernel, len(parts), pieces, count, first, at), (like(...  21.2 us
    ppermute x11, waiting for transfers between devices, along(): lax.ppermute(value, 'dp', [(at, (at + 2) % size) for at in range(size)])  17.1 us
    ppermute x12, starting transfers between devices, across(): return lax.ppermute(value, 'dp', [(at, at ^ 1) for at in range(self.size)])  13.4 us
    ppermute x18, starting transfers between devices, swap(): return lax.ppermute(value, 'tensor', [(at, at ^ bit) for at in range(size)])  13 us
    ppermute x12, waiting for transfers between devices, across(): return lax.ppermute(value, 'dp', [(at, at ^ 1) for at in range(self.size)])  12.9 us
  transfers between devices with their start and end apart: 44, of which 21 were waited for; matrix products, arithmetic and copies ran while one was open for 3% of the time, Pallas kernels for 34%

profile of v1, /device:TPU:0, one launch (start us, length us, event | category | flops | bytes accessed | tf_op | source)
XLA Modules:
  0.0 249.0 jit_solution(1519585889182646985)
XLA Ops:
  2.3 3.0 %collective-permute-start = (bf16[272,128]{1,0:T(8,128)(2,1)S(1)}, bf16[272,128]{1,0:T(8,128)(2,1)S(1)}, u32[]{:S(2)}, u32[]{:S(2)}) collective-permute-start(bf16[272,128]{1,0:T(8,128)(2,1)S(1)} %get-tuple-element.157), channel_id=1, source_target_pairs={{0,2},{1,3},{2,0},{3,1},{4,6},{5,7},{6,4},{7,5},{8,10},{9,11},{10,... | collective-permute-start | bytes 208904 | tf_op jit(solution)/shard_map/ppermute | solution.py:722
  5.4 2.3 collective-permute-done
  7.7 2.1 collective-permute-start.2
  21.5 4.9 %shard_map.258 = (bf16[416,512]{1,0:T(8,128)(2,1)}, f32[4,2,416]{2,1,0:T(2,128)}, s32[16,128]{1,0:T(8,128)}) custom-call(bf16[394,512]{1,0:T(8,128)(2,1)} %cot.1, s32[2,1664]{1,0:T(2,128)} %reshape.108.rflat, s32[4,2,416]{2,1,0:T(2,128)} %bitcast.71, s32[4,1,416]{2,1,0:T(1,128)} %transpose_reshape_reshape.3.prow, s32[1664,1]{1,0:T(8,128)} %transpose_reshape.4.pcol), custom_call_target="tpu_custom_call" | custom-call | flops 5500000256 | bytes 18000000 | tf_op jit(solution)/shard_map/pallas_call | solution.py:872
  32.3 2.3 collective-permute-done.7.refs_5_
  34.6 3.1 %collective-permute-done.8.refs_6_ = bf16[2,272,128]{2,1,0:T(8,128)(2,1)S(1)} collective-permute-done((bf16[2,272,128]{2,1,0:T(8,128)(2,1)S(1)}, bf16[2,272,128]{2,1,0:T(8,128)(2,1)S(1)}, u32[]{:S(2)}, u32[]{:S(2)}) %collective-permute-start.8) | collective-permute-done | bytes 139296 | tf_op jit(solution)/shard_map/ppermute | solution.py:770
  40.1 3.4 %collective-permute-done.11.refs_9_ = bf16[512,128]{1,0:T(8,128)(2,1)S(1)} collective-permute-done((bf16[512,128]{1,0:T(8,128)(2,1)S(1)}, bf16[512,128]{1,0:T(8,128)(2,1)S(1)}, u32[]{:S(2)}, u32[]{:S(2)}) %collective-permute-start.11) | collective-permute-done | bytes 131104 | tf_op jit(solution)/shard_map/ppermute | solution.py:722
  44.8 2.5 %shard_map.259 = (bf16[2,5,512,128]{3,2,1,0:T(8,128)(2,1)}, bf16[8,16,128]{2,1,0:T(8,128)(2,1)}) custom-call(bf16[2,272,128]{2,1,0:T(8,128)(2,1)} %copy-done.11, bf16[2,272,128]{2,1,0:T(8,128)(2,1)} %copy-done.48, bf16[2,272,128]{2,1,0:T(8,128)(2,1)} %copy-done.47, bf16[2,272,128]{2,1,0:T(8,128)(2,1)} %copy-done.50, bf16[2,272,128]{2,1,0:T(8,128)(2,1)} %copy-done.49, ...), custom_call_target="tpu_custom_call" | custom-call | flops 2200000000 | bytes 7200000 | tf_op jit(solution)/shard_map/pallas_call | solution.py:753
  51.7 9.7 %shard_map.260 = (bf16[5,512,512]{2,1,0:T(8,128)(2,1)}, f32[416,512]{1,0:T(8,128)}, bf16[416,512]{1,0:T(8,128)(2,1)}, bf16[416,384]{1,0:T(8,128)(2,1)}, bf16[416...) custom-call(s32[8]{0:T(128)} %adapter.5, ...), custom_call_target="tpu_custom_call" | custom-call | flops 11000000512 | bytes 36000000 | tf_op jit(solution)/shard_map/pallas_call | solution.py:90
  63.7 9.5 %collective-permute-done.24.refs_1_ = bf16[2,4,64,512]{3,2,1,0:T(8,128)(2,1)S(1)} collective-permute-done((bf16[2,4,64,512]{3,2,1,0:T(8,128)(2,1)S(1)}, bf16[2,4,64,512]{3,2,1,0:T(8,128)(2,1)S(1)}, u32[]{:S(2)}, u32[]{:S(2)}) %collective-permute-start.24) | collective-permute-done | bytes 524320 | tf_op jit(solution)/shard_map/ppermute | solution.py:773
  75.0 3.5 %collective-permute-done.23.refs_2_ = bf16[2,4,64,512]{3,2,1,0:T(8,128)(2,1)} collective-permute-done((bf16[2,4,64,512]{3,2,1,0:T(8,128)(2,1)S(1)}, bf16[2,4,64,512]{3,2,1,0:T(8,128)(2,1)}, u32[]{:S(2)}, u32[]{:S(2)}) %collective-permute-start.23) | collective-permute-done | bytes 524320 | tf_op jit(solution)/shard_map/ppermute | solution.py:770
  81.5 16.7 %shard_map.261 = (bf16[8,464,1152]{2,1,0:T(8,128)(2,1)}, bf16[4,416,512]{2,1,0:T(8,128)(2,1)}, bf16[4,416,128]{2,1,0:T(8,128)(2,1)}, f32[4,416,128]{2,1,0:T(8,128)}) custom-call(s32[8]{0:T(128)} %adapter.5, s32[16,128]{1,0:T(8,128)} %get-tuple-element.88.table.refs_17_, bf16[416,512]{1,0:T(8,128)(2,1)} %get-tuple-element.93.own, ...), custom_call_target="tpu_custom_call" | custom-call | flops 18699999232 | bytes 61200000 | tf_op jit(solution)/shard_map/pallas_call | solution.py:90
  102.4 4.0 %collective-permute-done.25.refs_4_ = bf16[2,4,64,512]{3,2,1,0:T(8,128)(2,1)S(1)} collective-permute-done((bf16[2,4,64,512]{3,2,1,0:T(8,128)(2,1)}, bf16[2,4,64,512]{3,2,1,0:T(8,128)(2,1)S(1)}, u32[]{:S(2)}, u32[]{:S(2)}) %collective-permute-start.25) | collective-permute-done | bytes 524320 | tf_op jit(solution)/shard_map/ppermute | solution.py:770
  106.4 5.6 %collective-permute-done.27.refs_7_ = bf16[2,2,64,512]{3,2,1,0:T(8,128)(2,1)S(1)} collective-permute-done((bf16[2,2,64,512]{3,2,1,0:T(8,128)(2,1)S(1)}, bf16[2,2,64,512]{3,2,1,0:T(8,128)(2,1)S(1)}, u32[]{:S(2)}, u32[]{:S(2)}) %collective-permute-start.27) | collective-permute-done | bytes 262176 | tf_op jit(solution)/shard_map/ppermute | solution.py:770
  113.4 10.4 %shard_map.262 = (bf16[2,464,640]{2,1,0:T(8,128)(2,1)}, bf16[2,464,512]{2,1,0:T(8,128)(2,1)}, f32[2,128,512]{2,1,0:T(8,128)}, f32[2,128,512]{2,1,0:T(8,128)}) custom-call(bf16[2,4,64,512]{3,2,1,0:T(8,128)(2,1)} %copy-done.4, bf16[2,4,64,512]{3,2,1,0:T(8,128)(2,1)} %copy-done.27, bf16[2,4,64,512]{3,2,1,0:T(8,128)(2,1)} %copy-done.26, ...), custom_call_target="tpu_custom_call" | custom-call | flops 8800000000 | bytes 28800000 | tf_op jit(solution)/shard_map/pallas_call | solution.py:957
  125.0 10.8 %shard_map.263 = (bf16[2,464,640]{2,1,0:T(8,128)(2,1)}, bf16[2,464,512]{2,1,0:T(8,128)(2,1)}, f32[2,128,512]{2,1,0:T(8,128)}, f32[2,128,512]{2,1,0:T(8,128)}) custom-call(bf16[2,4,64,512]{3,2,1,0:T(8,128)(2,1)} %copy-done.4, bf16[2,4,64,512]{3,2,1,0:T(8,128)(2,1)} %copy-done.27, bf16[2,4,64,512]{3,2,1,0:T(8,128)(2,1)} %copy-done.26, ...), custom_call_target="tpu_custom_call" | custom-call | flops 8800000000 | bytes 28800000 | tf_op jit(solution)/shard_map/pallas_call | solution.py:957
  136.6 28.8 %shard_map.264 = (bf16[4,464,512]{2,1,0:T(8,128)(2,1)}, bf16[2,416,512]{2,1,0:T(8,128)(2,1)}, bf16[2,416,512]{2,1,0:T(8,128)(2,1)}, bf16[8,96,512]{2,1,0:T(8,128)(2,1)}) custom-call(bf16[2,4,64,512]{3,2,1,0:T(8,128)(2,1)} %copy-done.5, bf16[2,4,64,512]{3,2,1,0:T(8,128)(2,1)} %copy-done.28, bf16[2,4,64,512]{3,2,1,0:T(8,128)(2,1)} %collective-permute-done.23.refs_2_, ...), custom_call_target="tpu_custom_call" | custom-call | flops 27499999232 | bytes 90000000 | tf_op jit(solution)/shard_map/pallas_call | solution.py:987
  165.5 2.6 %collective-permute-done.32.grad_b = bf16[2,416,512]{2,1,0:T(8,128)(2,1)S(1)} collective-permute-done((bf16[2,416,512]{2,1,0:T(8,128)(2,1)}, bf16[2,416,512]{2,1,0:T(8,128)(2,1)S(1)}, u32[]{:S(2)}, u32[]{:S(2)}) %collective-permute-start.32) | collective-permute-done | bytes 852000 | tf_op jit(solution)/shard_map/ppermute | solution.py:722
  170.1 5.8 %all-to-all-start.1 = ((bf16[8,96,512]{2,1,0:T(8,128)(2,1)}), bf16[8,96,512]{2,1,0:T(8,128)(2,1)S(1)}, u32[]{:S(2)}, u32[]{:S(2)}) async-start(bf16[8,96,512]{2,1,0:T(8,128)(2,1)} %get-tuple-element.138), calls=%async_computation.1 | async-start | bytes 1572864 | tf_op jit(solution)/shard_map/all_to_all | solution.py:1035
  175.9 7.5 %shard_map.265 = (bf16[2,416,512]{2,1,0:T(8,128)(2,1)}, bf16[2,416,512]{2,1,0:T(8,128)(2,1)}) custom-call(s32[16,128]{1,0:T(8,128)} %get-tuple-element.88.table.refs_17_, f32[4,416,2]{2,1,0:T(8,128)} %bitcast.62, bf16[2,464,512]{2,1,0:T(8,128)(2,1)} %get-tuple-element.99.refs_0_, bf16[2,464,512]{2,1,0:T(8,128)(2,1)} %get-tuple-element.106.refs_1_, ...), custom_call_target="tpu_custom_call" | custom-call | flops 7699999744 | bytes 25200000 | tf_op jit(solution)/shard_map/pallas_call | solution.py:1023
  184.1 11.7 %shard_map.266 = (f32[416,512]{1,0:T(8,128)}, bf16[416,1536]{1,0:T(8,128)(2,1)}, bf16[416,384]{1,0:T(8,128)(2,1)}, bf16[32,32,128]{2,1,0:T(8,128)(2,1)}) custom-call(s32[8]{0:T(128)} %adapter.5, bf16[416,512]{1,0:T(8,128)(2,1)} %get-tuple-element.118.dy_own.dy, f32[416,512]{1,0:T(8,128)} %get-tuple-element.129.middle, ...), custom_call_target="tpu_custom_call" | custom-call | flops 12099999744 | bytes 39600000 | tf_op jit(solution)/shard_map/pallas_call | solution.py:90
  196.1 5.8 %all-to-all-start = ((bf16[32,32,128]{2,1,0:T(8,128)(2,1)}), bf16[32,32,128]{2,1,0:T(8,128)(2,1)S(1)}, u32[]{:S(2)}, u32[]{:S(2)}) async-start(bf16[32,32,128]{2,1,0:T(8,128)(2,1)} %get-tuple-element.128), calls=%async_computation | async-start | bytes 524288 | tf_op jit(solution)/shard_map/all_to_all | solution.py:1054
  202.2 1.9 shard_map.269
  207.9 4.6 %all-to-all-done = bf16[32,32,128]{2,1,0:T(8,128)(2,1)S(1)} async-done(((bf16[32,32,128]{2,1,0:T(8,128)(2,1)}), bf16[32,32,128]{2,1,0:T(8,128)(2,1)S(1)}, u32[]{:S(2)}, u32[]{:S(2)}) %all-to-all-start) | async-done | bytes 262176 | tf_op jit(solution)/shard_map/all_to_all | solution.py:1054
  213.2 2.1 shard_map.270
  215.3 3.7 %all-to-all-start.2 = ((bf16[8,80,512]{2,1,0:T(8,128)(2,1)}), bf16[8,80,512]{2,1,0:T(8,128)(2,1)S(1)}, u32[]{:S(2)}, u32[]{:S(2)}) async-start(bf16[8,80,512]{2,1,0:T(8,128)(2,1)} %shard_map.270), calls=%async_computation.2 | async-start | bytes 1310720 | tf_op jit(solution)/shard_map/all_to_all | solution.py:1079
  220.2 5.4 %shard_map.268 = f32[394,512]{1,0:T(8,128)} custom-call(f32[416,512]{1,0:T(8,128)} %get-tuple-element.132.middle_grad, bf16[416,1536]{1,0:T(8,128)(2,1)} %get-tuple-element.133.proj_grad, bf16[416,384]{1,0:T(8,128)(2,1)} %get-tuple-element.134.code_grad, f32[416,512]{1,0:T(8,128)} %get-tuple-element.135.x_in, f32[2,512]{1,0:T(2,128)} %gain.5, ...), custom_call_target="tpu_custom_call" | custom-call | flops 5500000256 | bytes 18000000 | tf_op jit(solution)/shard_map/pallas_call | solution.py:1056
  225.6 5.2 %collective-permute-done.35.part_c = bf16[416,512]{1,0:T(8,128)(2,1)S(1)} collective-permute-done((bf16[416,512]{1,0:T(8,128)(2,1)S(1)}, bf16[416,512]{1,0:T(8,128)(2,1)S(1)}, u32[]{:S(2)}, u32[]{:S(2)}) %collective-permute-start.35) | collective-permute-done | bytes 426016 | tf_op jit(solution)/shard_map/ppermute | solution.py:722
  231.5 3.0 %shard_map.267 = f32[394,512]{1,0:T(8,128)} custom-call(f32[416,512]{1,0:T(8,128)} %get-tuple-element.129.middle, bf16[2,416,512]{2,1,0:T(8,128)(2,1)} %get-tuple-element.130.part_a, bf16[2,416,512]{2,1,0:T(8,128)(2,1)} %copy-done.9, bf16[416,512]{1,0:T(8,128)(2,1)} %copy-done.39), custom_call_target="tpu_custom_call" | custom-call | flops 2200000000 | bytes 7200000 | tf_op jit(solution)/shard_map/pallas_call | solution.py:1063
  234.5 2.0 all-to-all-done.2.came
  237.6 6.1 %collective-permute-done.39.side = bf16[256,512]{1,0:T(8,128)(2,1)S(1)} collective-permute-done((bf16[256,512]{1,0:T(8,128)(2,1)S(1)}, bf16[256,512]{1,0:T(8,128)(2,1)S(1)}, u32[]{:S(2)}, u32[]{:S(2)}) %collective-permute-start.39) | collective-permute-done | bytes 262176 | tf_op jit(solution)/shard_map/ppermute | solution.py:722
  245.9 3.0 %shard_map.271 = (f32[5,128,512]{2,1,0:T(8,128)}, f32[128,512]{1,0:T(8,128)}, f32[128,512]{1,0:T(8,128)}, f32[8,8,16]{2,1,0:T(8,128)}, f32[3,128,128]{2,1,0:T(8,...) custom-call(bf16[8,80,512]{2,1,0:T(8,128)(2,1)} %copy-done.2, bf16[256,512]{1,0:T(8,128)(2,1)} %copy-done.7, ...), custom_call_target="tpu_custom_call" | custom-call | flops 3300000000 | bytes 10800000 | tf_op jit(solution)/shard_map/pallas_call | solution.py:1088
  (220 shorter events, 54.7 us)
Async XLA Ops:
  7.7 10.7 %collective-permute-start.2 = (bf16[2,272,128]{2,1,0:T(8,128)(2,1)S(1)}, bf16[2,272,128]{2,1,0:T(8,128)(2,1)S(1)}, u32[]{:S(2)}, u32[]{:S(2)}) collective-permute-start(bf16[2,272,128]{2,1,0:T(8,128)(2,1)S(1)} %pad_maximum_fusion.3.refs_0_), channel_id=1, source_target_pairs={{0,8},{4,12},{8,16},{12,20},{16,24},{20,28},{24,0},{28,4},{1,9},{5... | collective-permute-start | bytes 417800 | tf_op jit(solution)/shard_map/ppermute | solution.py:770
  9.8 8.5 %collective-permute-start.1 = (bf16[2,272,128]{2,1,0:T(8,128)(2,1)S(1)}, bf16[2,272,128]{2,1,0:T(8,128)(2,1)S(1)}, u32[]{:S(2)}, u32[]{:S(2)}) collective-permute-start(bf16[2,272,128]{2,1,0:T(8,128)(2,1)S(1)} %pad_maximum_fusion.3.refs_0_), channel_id=1, source_target_pairs={{0,4},{4,0},{8,12},{12,8},{16,20},{20,16},{24,28},{28,24},{1,5},{5... | collective-permute-start | bytes 417800 | tf_op jit(solution)/shard_map/ppermute | solution.py:773
  12.7 16.8 %collective-permute-start.5 = (bf16[2,4,64,512]{3,2,1,0:T(8,128)(2,1)S(1)}, bf16[2,4,64,512]{3,2,1,0:T(8,128)(2,1)S(1)}, u32[]{:S(2)}, u32[]{:S(2)}) collective-permute-start(bf16[2,4,64,512]{3,2,1,0:T(8,128)(2,1)S(1)} %pad_maximum_fusion.refs_0_), channel_id=1, source_target_pairs={{0,8},{4,12},{8,16},{12,20},{16,24},{20,28},{24,0},{28,4},{1,9},{5... | collective-permute-start | bytes 1572872 | tf_op jit(solution)/shard_map/ppermute | solution.py:770
  14.3 15.2 %collective-permute-start.6 = (bf16[2,4,64,512]{3,2,1,0:T(8,128)(2,1)S(1)}, bf16[2,4,64,512]{3,2,1,0:T(8,128)(2,1)S(1)}, u32[]{:S(2)}, u32[]{:S(2)}) collective-permute-start(bf16[2,4,64,512]{3,2,1,0:T(8,128)(2,1)S(1)} %pad_maximum_fusion.refs_0_), channel_id=1, source_target_pairs={{0,4},{4,0},{8,12},{12,8},{16,20},{20,16},{24,28},{28,24},{1,5},{5... | collective-permute-start | bytes 1572872 | tf_op jit(solution)/shard_map/ppermute | solution.py:773
  18.4 11.1 %collective-permute-start.4 = (bf16[2,272,128]{2,1,0:T(8,128)(2,1)S(1)}, bf16[2,272,128]{2,1,0:T(8,128)(2,1)S(1)}, u32[]{:S(2)}, u32[]{:S(2)}) collective-permute-start(bf16[2,272,128]{2,1,0:T(8,128)(2,1)S(1)} %collective-permute-done.2.refs_2_), channel_id=1, source_target_pairs={{0,8},{4,12},{8,16},{12,20},{16,24},{20,28},{24,0},{28,4},{1,9},{5... | collective-permute-start | bytes 417800 | tf_op jit(solution)/shard_map/ppermute | solution.py:770
  20.0 9.1 %collective-permute-start.3 = (bf16[2,272,128]{2,1,0:T(8,128)(2,1)S(1)}, bf16[2,272,128]{2,1,0:T(8,128)(2,1)S(1)}, u32[]{:S(2)}, u32[]{:S(2)}) collective-permute-start(bf16[2,272,128]{2,1,0:T(8,128)(2,1)S(1)} %collective-permute-done.2.refs_2_), channel_id=1, source_target_pairs={{0,4},{4,0},{8,12},{12,8},{16,20},{20,16},{24,28},{28,24},{1,5},{5... | collective-permute-start | bytes 417800 | tf_op jit(solution)/shard_map/ppermute | solution.py:773
  26.5 13.6 %collective-permute-start.10 = (bf16[416,512]{1,0:T(8,128)(2,1)}, bf16[416,512]{1,0:T(8,128)(2,1)S(1)}, u32[]{:S(2)}, u32[]{:S(2)}) collective-permute-start(bf16[416,512]{1,0:T(8,128)(2,1)} %get-tuple-element.118.dy_own.dy), channel_id=1, source_target_pairs={{0,2},{1,3},{2,0},{3,1},{4,6},{5,7},{6,4},{7,5},{8,10},{9,11},{10,... | collective-permute-start | bytes 1277960 | tf_op jit(solution)/shard_map/ppermute | solution.py:722
  47.5 16.2 %collective-permute-start.14 = (bf16[2,4,64,512]{3,2,1,0:T(8,128)(2,1)S(1)}, bf16[2,4,64,512]{3,2,1,0:T(8,128)(2,1)S(1)}, u32[]{:S(2)}, u32[]{:S(2)}) collective-permute-start(bf16[2,4,64,512]{3,2,1,0:T(8,128)(2,1)S(1)} %collective-permute-done.5.refs_2_), channel_id=1, source_target_pairs={{0,8},{4,12},{8,16},{12,20},{16,24},{20,28},{24,0},{28,4},{1,9},{5... | collective-permute-start | bytes 1572872 | tf_op jit(solution)/shard_map/ppermute | solution.py:770
  47.5 15.5 %collective-permute-start.13 = (bf16[2,4,64,512]{3,2,1,0:T(8,128)(2,1)S(1)}, bf16[2,4,64,512]{3,2,1,0:T(8,128)(2,1)S(1)}, u32[]{:S(2)}, u32[]{:S(2)}) collective-permute-start(bf16[2,4,64,512]{3,2,1,0:T(8,128)(2,1)S(1)} %collective-permute-done.5.refs_2_), channel_id=1, source_target_pairs={{0,4},{4,0},{8,12},{12,8},{16,20},{20,16},{24,28},{28,24},{1,5},{5... | collective-permute-start | bytes 1572872 | tf_op jit(solution)/shard_map/ppermute | solution.py:773
  48.9 24.2 %collective-permute-start.24 = (bf16[2,4,64,512]{3,2,1,0:T(8,128)(2,1)S(1)}, bf16[2,4,64,512]{3,2,1,0:T(8,128)(2,1)S(1)}, u32[]{:S(2)}, u32[]{:S(2)}) collective-permute-start(bf16[2,4,64,512]{3,2,1,0:T(8,128)(2,1)S(1)} %pad_maximum_fusion.1.refs_0_), channel_id=1, source_target_pairs={{0,4},{4,0},{8,12},{12,8},{16,20},{20,16},{24,28},{28,24},{1,5},{5... | collective-permute-start | bytes 1572872 | tf_op jit(solution)/shard_map/ppermute | solution.py:773
  61.4 12.2 %collective-permute-start.18 = (bf16[416,512]{1,0:T(8,128)(2,1)}, bf16[416,512]{1,0:T(8,128)(2,1)}, u32[]{:S(2)}, u32[]{:S(2)}) collective-permute-start(bf16[416,512]{1,0:T(8,128)(2,1)} %get-tuple-element.93.own), channel_id=1, source_target_pairs={{0,2},{1,3},{2,0},{3,1},{4,6},{5,7},{6,4},{7,5},{8,10},{9,11},{10,... | collective-permute-start | bytes 1277960 | tf_op jit(solution)/shard_map/ppermute | solution.py:722
  62.9 15.6 %collective-permute-start.23 = (bf16[2,4,64,512]{3,2,1,0:T(8,128)(2,1)S(1)}, bf16[2,4,64,512]{3,2,1,0:T(8,128)(2,1)}, u32[]{:S(2)}, u32[]{:S(2)}) collective-permute-start(bf16[2,4,64,512]{3,2,1,0:T(8,128)(2,1)S(1)} %pad_maximum_fusion.1.refs_0_), channel_id=1, source_target_pairs={{0,8},{4,12},{8,16},{12,20},{16,24},{20,28},{24,0},{28,4},{1,9},{5... | collective-permute-start | bytes 1572872 | tf_op jit(solution)/shard_map/ppermute | solution.py:770
  63.0 15.5 %collective-permute-start.20 = (bf16[416,512]{1,0:T(8,128)(2,1)S(1)}, bf16[416,512]{1,0:T(8,128)(2,1)S(1)}, u32[]{:S(2)}, u32[]{:S(2)}) collective-permute-start(bf16[416,512]{1,0:T(8,128)(2,1)S(1)} %copy-done.32), channel_id=1, source_target_pairs={{0,1},{1,0},{2,3},{3,2},{4,5},{5,4},{6,7},{7,6},{8,9},{9,8},{10,11... | collective-permute-start | bytes 1277960 | tf_op jit(solution)/shard_map/ppermute | solution.py:722
  63.6 16.3 %collective-permute-start.21 = (bf16[416,512]{1,0:T(8,128)(2,1)S(1)}, bf16[416,512]{1,0:T(8,128)(2,1)S(1)}, u32[]{:S(2)}, u32[]{:S(2)}) collective-permute-start(bf16[416,512]{1,0:T(8,128)(2,1)S(1)} %collective-permute-done.10.dy_side), channel_id=1, source_target_pairs={{0,1},{1,0},{2,3},{3,2},{4,5},{5,4},{6,7},{7,6},{8,9},{9,8},{10,11... | collective-permute-start | bytes 1277960 | tf_op jit(solution)/shard_map/ppermute | solution.py:722
  73.5 7.2 %collective-permute-start.19 = (bf16[416,512]{1,0:T(8,128)(2,1)}, bf16[416,512]{1,0:T(8,128)(2,1)S(1)}, u32[]{:S(2)}, u32[]{:S(2)}) collective-permute-start(bf16[416,512]{1,0:T(8,128)(2,1)} %collective-permute-done.18.side), channel_id=1, source_target_pairs={{0,1},{1,0},{2,3},{3,2},{4,5},{5,4},{6,7},{7,6},{8,9},{9,8},{10,11... | collective-permute-start | bytes 1277960 | tf_op jit(solution)/shard_map/ppermute | solution.py:722
  78.5 21.2 %collective-permute-start.16 = (bf16[2,4,64,512]{3,2,1,0:T(8,128)(2,1)S(1)}, bf16[2,4,64,512]{3,2,1,0:T(8,128)(2,1)S(1)}, u32[]{:S(2)}, u32[]{:S(2)}) collective-permute-start(bf16[2,4,64,512]{3,2,1,0:T(8,128)(2,1)S(1)} %collective-permute-done.14.refs_4_), channel_id=1, source_target_pairs={{0,8},{4,12},{8,16},{12,20},{16,24},{20,28},{24,0},{28,4},{1,9},{5... | collective-permute-start | bytes 1572872 | tf_op jit(solution)/shard_map/ppermute | solution.py:770
  78.5 19.6 %collective-permute-start.15 = (bf16[2,4,64,512]{3,2,1,0:T(8,128)(2,1)S(1)}, bf16[2,4,64,512]{3,2,1,0:T(8,128)(2,1)S(1)}, u32[]{:S(2)}, u32[]{:S(2)}) collective-permute-start(bf16[2,4,64,512]{3,2,1,0:T(8,128)(2,1)S(1)} %collective-permute-done.14.refs_4_), channel_id=1, source_target_pairs={{0,4},{4,0},{8,12},{12,8},{16,20},{20,16},{24,28},{28,24},{1,5},{5... | collective-permute-start | bytes 1572872 | tf_op jit(solution)/shard_map/ppermute | solution.py:773
  79.9 26.5 %collective-permute-start.25 = (bf16[2,4,64,512]{3,2,1,0:T(8,128)(2,1)}, bf16[2,4,64,512]{3,2,1,0:T(8,128)(2,1)S(1)}, u32[]{:S(2)}, u32[]{:S(2)}) collective-permute-start(bf16[2,4,64,512]{3,2,1,0:T(8,128)(2,1)} %collective-permute-done.23.refs_2_), channel_id=1, source_target_pairs={{0,8},{4,12},{8,16},{12,20},{16,24},{20,28},{24,0},{28,4},{1,9},{5... | collective-permute-start | bytes 1572872 | tf_op jit(solution)/shard_map/ppermute | solution.py:770
  79.9 26.4 %collective-permute-start.26 = (bf16[2,4,64,512]{3,2,1,0:T(8,128)(2,1)}, bf16[2,4,64,512]{3,2,1,0:T(8,128)(2,1)}, u32[]{:S(2)}, u32[]{:S(2)}) collective-permute-start(bf16[2,4,64,512]{3,2,1,0:T(8,128)(2,1)} %collective-permute-done.23.refs_2_), channel_id=1, source_target_pairs={{0,4},{4,0},{8,12},{12,8},{16,20},{20,16},{24,28},{28,24},{1,5},{5... | collective-permute-start | bytes 1572872 | tf_op jit(solution)/shard_map/ppermute | solution.py:773
  98.2 13.8 %collective-permute-start.27 = (bf16[2,2,64,512]{3,2,1,0:T(8,128)(2,1)S(1)}, bf16[2,2,64,512]{3,2,1,0:T(8,128)(2,1)S(1)}, u32[]{:S(2)}, u32[]{:S(2)}) collective-permute-start(bf16[2,2,64,512]{3,2,1,0:T(8,128)(2,1)S(1)} %slice.53), channel_id=1, source_target_pairs={{0,8},{4,12},{8,16},{12,20},{16,24},{20,28},{24,0},{28,4},{1,9},{5... | collective-permute-start | bytes 786440 | tf_op jit(solution)/shard_map/ppermute | solution.py:770
  99.7 12.3 %collective-permute-start.22 = (bf16[2,2,64,512]{3,2,1,0:T(8,128)(2,1)S(1)}, bf16[2,2,64,512]{3,2,1,0:T(8,128)(2,1)S(1)}, u32[]{:S(2)}, u32[]{:S(2)}) collective-permute-start(bf16[2,2,64,512]{3,2,1,0:T(8,128)(2,1)S(1)} %slice.50), channel_id=1, source_target_pairs={{0,4},{4,0},{8,12},{12,8},{16,20},{20,16},{24,28},{28,24},{1,5},{5... | collective-permute-start | bytes 786440 | tf_op jit(solution)/shard_map/ppermute | solution.py:773
  106.4 17.5 %collective-permute-start.28 = (bf16[2,4,64,512]{3,2,1,0:T(8,128)(2,1)S(1)}, bf16[2,4,64,512]{3,2,1,0:T(8,128)(2,1)S(1)}, u32[]{:S(2)}, u32[]{:S(2)}) collective-permute-start(bf16[2,4,64,512]{3,2,1,0:T(8,128)(2,1)S(1)} %collective-permute-done.25.refs_4_), channel_id=1, source_target_pairs={{0,8},{4,12},{8,16},{12,20},{16,24},{20,28},{24,0},{28,4},{1,9},{5... | collective-permute-start | bytes 1572872 | tf_op jit(solution)/shard_map/ppermute | solution.py:770
  112.0 12.7 %collective-permute-start.29 = (bf16[2,4,64,512]{3,2,1,0:T(8,128)(2,1)S(1)}, bf16[2,4,64,512]{3,2,1,0:T(8,128)(2,1)S(1)}, u32[]{:S(2)}, u32[]{:S(2)}) collective-permute-start(bf16[2,4,64,512]{3,2,1,0:T(8,128)(2,1)S(1)} %collective-permute-done.25.refs_4_), channel_id=1, source_target_pairs={{0,4},{4,0},{8,12},{12,8},{16,20},{20,16},{24,28},{28,24},{1,5},{5... | collective-permute-start | bytes 1572872 | tf_op jit(solution)/shard_map/ppermute | solution.py:773
  123.9 11.9 %collective-permute-start.30 = (bf16[2,2,64,512]{3,2,1,0:T(8,128)(2,1)S(1)}, bf16[2,2,64,512]{3,2,1,0:T(8,128)(2,1)S(1)}, u32[]{:S(2)}, u32[]{:S(2)}) collective-permute-start(bf16[2,2,64,512]{3,2,1,0:T(8,128)(2,1)S(1)} %slice.54), channel_id=1, source_target_pairs={{0,4},{4,0},{8,12},{12,8},{16,20},{20,16},{24,28},{28,24},{1,5},{5... | collective-permute-start | bytes 786440 | tf_op jit(solution)/shard_map/ppermute | solution.py:773
  124.7 11.1 %collective-permute-start.31 = (bf16[2,2,64,512]{3,2,1,0:T(8,128)(2,1)S(1)}, bf16[2,2,64,512]{3,2,1,0:T(8,128)(2,1)S(1)}, u32[]{:S(2)}, u32[]{:S(2)}) collective-permute-start(bf16[2,2,64,512]{3,2,1,0:T(8,128)(2,1)S(1)} %slice.55), channel_id=1, source_target_pairs={{0,8},{4,12},{8,16},{12,20},{16,24},{20,28},{24,0},{28,4},{1,9},{5... | collective-permute-start | bytes 786440 | tf_op jit(solution)/shard_map/ppermute | solution.py:770
  169.5 13.9 %collective-permute-start.33 = (bf16[416,512]{1,0:T(8,128)(2,1)S(1)}, bf16[416,512]{1,0:T(8,128)(2,1)S(1)}, u32[]{:S(2)}, u32[]{:S(2)}) collective-permute-start(bf16[416,512]{1,0:T(8,128)(2,1)S(1)} %fusion), channel_id=1, source_target_pairs={{0,2},{1,3},{2,0},{3,1},{4,6},{5,7},{6,4},{7,5},{8,10},{9,11},{10,... | collective-permute-start | bytes 1277960 | tf_op jit(solution)/shard_map/ppermute | solution.py:722
  170.1 26.0 %all-to-all-start.1 = ((bf16[8,96,512]{2,1,0:T(8,128)(2,1)}), bf16[8,96,512]{2,1,0:T(8,128)(2,1)S(1)}, u32[]{:S(2)}, u32[]{:S(2)}) async-start(bf16[8,96,512]{2,1,0:T(8,128)(2,1)} %get-tuple-element.138), calls=%async_computation.1 | async-start | bytes 1572864 | tf_op jit(solution)/shard_map/all_to_all | solution.py:1035
  196.1 16.4 %all-to-all-start = ((bf16[32,32,128]{2,1,0:T(8,128)(2,1)}), bf16[32,32,128]{2,1,0:T(8,128)(2,1)S(1)}, u32[]{:S(2)}, u32[]{:S(2)}) async-start(bf16[32,32,128]{2,1,0:T(8,128)(2,1)} %get-tuple-element.128), calls=%async_computation | async-start | bytes 524288 | tf_op jit(solution)/shard_map/all_to_all | solution.py:1054
  201.9 17.1 %collective-permute-start.34 = (bf16[2,416,512]{2,1,0:T(8,128)(2,1)S(1)}, bf16[2,416,512]{2,1,0:T(8,128)(2,1)S(1)}, u32[]{:S(2)}, u32[]{:S(2)}) collective-permute-start(bf16[2,416,512]{2,1,0:T(8,128)(2,1)S(1)} %copy-done.25), channel_id=1, source_target_pairs={{0,1},{1,0},{2,3},{3,2},{4,5},{5,4},{6,7},{7,6},{8,9},{9,8},{10,11... | collective-permute-start | bytes 2555912 | tf_op jit(solution)/shard_map/ppermute | solution.py:722
  215.3 21.3 %all-to-all-start.2 = ((bf16[8,80,512]{2,1,0:T(8,128)(2,1)}), bf16[8,80,512]{2,1,0:T(8,128)(2,1)S(1)}, u32[]{:S(2)}, u32[]{:S(2)}) async-start(bf16[8,80,512]{2,1,0:T(8,128)(2,1)} %shard_map.270), calls=%async_computation.2 | async-start | bytes 1310720 | tf_op jit(solution)/shard_map/all_to_all | solution.py:1079
  219.1 11.7 %collective-permute-start.35 = (bf16[416,512]{1,0:T(8,128)(2,1)S(1)}, bf16[416,512]{1,0:T(8,128)(2,1)S(1)}, u32[]{:S(2)}, u32[]{:S(2)}) collective-permute-start(bf16[416,512]{1,0:T(8,128)(2,1)S(1)} %fusion.1), channel_id=1, source_target_pairs={{0,2},{1,3},{2,0},{3,1},{4,6},{5,7},{6,4},{7,5},{8,10},{9,11},{10,... | collective-permute-start | bytes 1277960 | tf_op jit(solution)/shard_map/ppermute | solution.py:722
  236.6 7.0 %collective-permute-start.39 = (bf16[256,512]{1,0:T(8,128)(2,1)S(1)}, bf16[256,512]{1,0:T(8,128)(2,1)S(1)}, u32[]{:S(2)}, u32[]{:S(2)}) collective-permute-start(bf16[256,512]{1,0:T(8,128)(2,1)S(1)} %pad_maximum_fusion.2.own), channel_id=1, source_target_pairs={{0,2},{1,3},{2,0},{3,1},{4,6},{5,7},{6,4},{7,5},{8,10},{9,11},{10,... | collective-permute-start | bytes 786440 | tf_op jit(solution)/shard_map/ppermute | solution.py:722
  (68 other events, 614.7 us)

commit v2 on v1

--- a/solution.py
+++ b/solution.py
@@ -72,7 +72,7 @@
 
 
 def call(
-    body, outs, scratch=(), smem=0, grid=None, in_specs=None, out_specs=None, cost=None, vmem=56
+    body, outs, scratch=(), smem=0, grid=None, in_specs=None, out_specs=None, cost=None, vmem=16
 ):
     options = {}
     if grid is not None:
@@ -282,7 +282,7 @@
 
 
 def dispatch_kernel(
-    adapter, table, own, core, side, both, dy_own, dy_core, dy_side, dy_both,
+    adapter, table, own, core, side, both, dy_near, dy_far,
     place, down, router, up_router,
     slots, normed_out, rcode_out, prob_out, rows, packed,
 ):
@@ -291,7 +291,10 @@
     width = own.shape[1]
     lane = lanes((1, 128))
     for index, (part, dy) in enumerate(
-        ((own, dy_own), (core, dy_core), (side, dy_side), (both, dy_both))
+        (
+            (own, dy_near.at[0]), (core, dy_far.at[0]),
+            (side, dy_near.at[1]), (both, dy_far.at[1]),
+        )
     ):
         normed_out[index] = part[...]
         rows[index, :, 0:width] = part[...]
@@ -879,8 +882,10 @@
         scratch=[pltpu.VMEM((count, width), F32)],
         cost=cost(5),
     )(cotangent, route_row, by_chunk(route_row), by_chunk(rank_row), rank_row.T)
-    dy_four = gather_four(dy)
-    begun, mine, ids = gather_projections(block, extra, ids, (dy_four[2],) + early_ring.done)
+    dy_side = swap(dy, 2)
+    dy_near = jnp.stack([dy, dy_side])
+    dy_far = swap(dy_near, 1)
+    begun, mine, ids = gather_projections(block, extra, ids, (dy_side,) + early_ring.done)
     early_ring.step(*begun[1])
     late_ring = gather(after(late_block, *begun[2]))
     late_ring.step()
@@ -929,7 +934,8 @@
         ],
         smem=2,
         cost=cost(17),
-    )(adapter_index, table, *normed2_four, *dy_four, place, down, router, router_up)
+        vmem=56,
+    )(adapter_index, table, *normed2_four, dy_near, dy_far, place, down, router, router_up)
 
     part = base // 2
     common, near, far = early_ring.finish(slots, split=part)
@@ -967,6 +973,7 @@
             in_specs=[hbm] * len(parts) + [each(row_wide, at)] + small + sums[: len(before)],
             out_specs=(each(grad_wide, 0), each(width, 0), *sums),
             cost=cost(4 * count),
+            vmem=56,
         )(*parts, slots, up_hid, down_hid, up_exo, down, *before)
 
     near, pieces = ([near], (0,)) if fits else ([], ())
@@ -1016,6 +1023,7 @@
             whole(8, 96, width) if compact else whole(6, CODE, width),
         ),
         cost=cost(25),
+        vmem=56,
     )(
         *last_parts, slots, up_hid, down_hid, up_exo, down, *before,
         adapter_index, table, place, router, router_up, grad_a, grad_b, rows, rcode, probs,
@@ -1027,6 +1035,7 @@
         in_specs=[smem] + [vmem] * 4,
         out_specs=(vmem, vmem),
         cost=cost(7),
+        vmem=56,
     )(table, place, mix_a, mix_b, mix_c)
 
     both = ("dp", "tensor")

time: 250 us -> 241 us (0.964)
  Pallas kernels: 118 us -> 108 us
  waiting for transfers between devices: 60.5 us -> 68.5 us
  local copies, waits for them, and re-layouts: 14.6 us -> 10.4 us
    ppermute x18 -> x17, waiting for transfers between devices: 23.6 us -> 32.9 us  [swap(): return lax.ppermute(value, 'tensor', [(at, at ^ bit) for at in range(size)])]
    ppermute x11, waiting for transfers between devices: 17.1 us -> 13.7 us  [along(): lax.ppermute(value, 'dp', [(at, (at + 2) % size) for at in range(size)])]
    all_to_all x1, waiting for transfers between devices: 1.99 us -> 4.51 us  [per_device(): came = lax.all_to_all(packed, 'dp', 0, 0)]
    unnamed x112 -> x68, local copies, waits for them, and re-layouts: 6.96 us -> 5.44 us
    ppermute x18 -> x17, starting transfers between devices: 13 us -> 12.6 us  [swap(): return lax.ppermute(value, 'tensor', [(at, at ^ bit) for at in range(size)])]
  transfers between devices with their start and end apart: 44 -> 43, of which waited for: 21 -> 21; matrix products, arithmetic and copies ran while one was open for 3% -> 2% of each run, Pallas kernels for 34% -> 32%
where the time goes in v2:
time: 241 us
  Pallas kernels  108 us (45%)
  waiting for transfers between devices  68.5 us (28%)
  starting transfers between devices  49.2 us (20%)
  local copies, waits for them, and re-layouts  10.4 us (4%)
  other arithmetic  3.27 us (1%)
    pallas_call x3, Pallas kernels, build(): return call(body, outs, scratch, 0, None, specs, ends, cost, vmem)(*args)  37.8 us
    ppermute x17, waiting for transfers between devices, swap(): return lax.ppermute(value, 'tensor', [(at, at ^ bit) for at in range(size)])  32.9 us
    pallas_call x1, Pallas kernels, per_device(): call(partial(last_kernel, len(last_parts), pieces, count_last, 0, base),...  28.8 us
    pallas_call x2, Pallas kernels, experts(): call(partial(expert_kernel, len(parts), pieces, count, first, at), (like(...  21.2 us
    ppermute x11, waiting for transfers between devices, along(): lax.ppermute(value, 'dp', [(at, (at + 2) % size) for at in range(size)])  13.7 us
    ppermute x12, starting transfers between devices, across(): return lax.ppermute(value, 'dp', [(at, at ^ 1) for at in range(self.size)])  13.6 us
    ppermute x17, starting transfers between devices, swap(): return lax.ppermute(value, 'tensor', [(at, at ^ bit) for at in range(size)])  12.6 us
    ppermute x12, waiting for transfers between devices, across(): return lax.ppermute(value, 'dp', [(at, at ^ 1) for at in range(self.size)])  10.8 us
  transfers between devices with their start and end apart: 43, of which 21 were waited for; matrix products, arithmetic and copies ran while one was open for 2% of the time, Pallas kernels for 32%

profile of v2, /device:TPU:0, one launch (start us, length us, event | category | flops | bytes accessed | tf_op | source)
XLA Modules:
  0.0 240.5 jit_solution(7251635238032198141)
XLA Ops:
  2.3 3.0 %collective-permute-start = (bf16[272,128]{1,0:T(8,128)(2,1)S(1)}, bf16[272,128]{1,0:T(8,128)(2,1)S(1)}, u32[]{:S(2)}, u32[]{:S(2)}) collective-permute-start(bf16[272,128]{1,0:T(8,128)(2,1)S(1)} %get-tuple-element.157), channel_id=1, source_target_pairs={{0,2},{1,3},{2,0},{3,1},{4,6},{5,7},{6,4},{7,5},{8,10},{9,11},{10,... | collective-permute-start | bytes 208904 | tf_op jit(solution)/shard_map/ppermute | solution.py:725
  5.4 2.3 collective-permute-done
  7.7 2.1 collective-permute-start.2
  17.4 1.8 collective-permute-start.3
  19.1 2.9 %shard_map.258 = (bf16[416,512]{1,0:T(8,128)(2,1)S(1)}, f32[4,2,416]{2,1,0:T(2,128)S(1)}, s32[16,128]{1,0:T(8,128)S(1)}) custom-call(bf16[394,512]{1,0:T(8,128)(2,1)S(1)} %copy-done.7, s32[2,1664]{1,0:T(2,128)S(1)} %reshape.108.rflat, s32[4,2,416]{2,1,0:T(2,128)S(1)} %bitcast.65, s32[4,1,416]{2,1,0:T(1,128)S(1)} %transpose_reshape_reshape.3.prow, ...), custom_call_target="tpu_custom_call" | custom-call | flops 5500000256 | bytes 18000000 | tf_op jit(solution)/shard_map/pallas_call | solution.py:875
  24.8 4.3 %collective-permute-done.3.refs_3_ = bf16[2,272,128]{2,1,0:T(8,128)(2,1)S(1)} collective-permute-done((bf16[2,272,128]{2,1,0:T(8,128)(2,1)S(1)}, bf16[2,272,128]{2,1,0:T(8,128)(2,1)S(1)}, u32[]{:S(2)}, u32[]{:S(2)}) %collective-permute-start.3) | collective-permute-done | bytes 139296 | tf_op jit(solution)/shard_map/ppermute | solution.py:776
  32.3 2.3 collective-permute-done.7.refs_5_
  34.6 3.1 %collective-permute-done.8.refs_6_ = bf16[2,272,128]{2,1,0:T(8,128)(2,1)S(1)} collective-permute-done((bf16[2,272,128]{2,1,0:T(8,128)(2,1)S(1)}, bf16[2,272,128]{2,1,0:T(8,128)(2,1)S(1)}, u32[]{:S(2)}, u32[]{:S(2)}) %collective-permute-start.8) | collective-permute-done | bytes 139296 | tf_op jit(solution)/shard_map/ppermute | solution.py:773
  40.0 3.4 %collective-permute-done.11.refs_9_ = bf16[512,128]{1,0:T(8,128)(2,1)S(1)} collective-permute-done((bf16[512,128]{1,0:T(8,128)(2,1)S(1)}, bf16[512,128]{1,0:T(8,128)(2,1)S(1)}, u32[]{:S(2)}, u32[]{:S(2)}) %collective-permute-start.11) | collective-permute-done | bytes 131104 | tf_op jit(solution)/shard_map/ppermute | solution.py:725
  47.8 9.6 %shard_map.260 = (bf16[5,512,512]{2,1,0:T(8,128)(2,1)}, f32[416,512]{1,0:T(8,128)}, bf16[416,512]{1,0:T(8,128)(2,1)}, bf16[416,384]{1,0:T(8,128)(2,1)}, bf16[416...) custom-call(s32[8]{0:T(128)} %adapter.5, ...), custom_call_target="tpu_custom_call" | custom-call | flops 11000000512 | bytes 36000000 | tf_op jit(solution)/shard_map/pallas_call | solution.py:90
  61.8 7.8 %collective-permute-done.18.side = bf16[416,512]{1,0:T(8,128)(2,1)} collective-permute-done((bf16[416,512]{1,0:T(8,128)(2,1)}, bf16[416,512]{1,0:T(8,128)(2,1)}, u32[]{:S(2)}, u32[]{:S(2)}) %collective-permute-start.18) | collective-permute-done | bytes 426016 | tf_op jit(solution)/shard_map/ppermute | solution.py:725
  70.9 2.8 %collective-permute-done.23.refs_1_ = bf16[2,4,64,512]{3,2,1,0:T(8,128)(2,1)} collective-permute-done((bf16[2,4,64,512]{3,2,1,0:T(8,128)(2,1)S(1)}, bf16[2,4,64,512]{3,2,1,0:T(8,128)(2,1)}, u32[]{:S(2)}, u32[]{:S(2)}) %collective-permute-start.23) | collective-permute-done | bytes 524320 | tf_op jit(solution)/shard_map/ppermute | solution.py:776
  73.7 2.9 %collective-permute-done.22.refs_2_ = bf16[2,4,64,512]{3,2,1,0:T(8,128)(2,1)} collective-permute-done((bf16[2,4,64,512]{3,2,1,0:T(8,128)(2,1)S(1)}, bf16[2,4,64,512]{3,2,1,0:T(8,128)(2,1)}, u32[]{:S(2)}, u32[]{:S(2)}) %collective-permute-start.22) | collective-permute-done | bytes 524320 | tf_op jit(solution)/shard_map/ppermute | solution.py:773
  79.4 16.5 %shard_map.261 = (bf16[8,464,1152]{2,1,0:T(8,128)(2,1)}, bf16[4,416,512]{2,1,0:T(8,128)(2,1)}, bf16[4,416,128]{2,1,0:T(8,128)(2,1)}, f32[4,416,128]{2,1,0:T(8,128)}) custom-call(s32[8]{0:T(128)} %adapter.5, s32[16,128]{1,0:T(8,128)} %copy-done.9, bf16[416,512]{1,0:T(8,128)(2,1)} %get-tuple-element.93.own, bf16[416,512]{1,0:T(8,128)(2,1)} %copy-done.28, ...), custom_call_target="tpu_custom_call" | custom-call | flops 18699999232 | bytes 61200000 | tf_op jit(solution)/shard_map/pallas_call | solution.py:90
  98.5 3.1 %collective-permute-done.24.refs_4_ = bf16[2,4,64,512]{3,2,1,0:T(8,128)(2,1)S(1)} collective-permute-done((bf16[2,4,64,512]{3,2,1,0:T(8,128)(2,1)}, bf16[2,4,64,512]{3,2,1,0:T(8,128)(2,1)S(1)}, u32[]{:S(2)}, u32[]{:S(2)}) %collective-permute-start.24) | collective-permute-done | bytes 524320 | tf_op jit(solution)/shard_map/ppermute | solution.py:773
  102.9 4.3 %collective-permute-done.26.refs_7_ = bf16[2,2,64,512]{3,2,1,0:T(8,128)(2,1)S(1)} collective-permute-done((bf16[2,2,64,512]{3,2,1,0:T(8,128)(2,1)S(1)}, bf16[2,2,64,512]{3,2,1,0:T(8,128)(2,1)S(1)}, u32[]{:S(2)}, u32[]{:S(2)}) %collective-permute-start.26) | collective-permute-done | bytes 262176 | tf_op jit(solution)/shard_map/ppermute | solution.py:773
  108.7 10.4 %shard_map.262 = (bf16[2,464,640]{2,1,0:T(8,128)(2,1)}, bf16[2,464,512]{2,1,0:T(8,128)(2,1)}, f32[2,128,512]{2,1,0:T(8,128)}, f32[2,128,512]{2,1,0:T(8,128)}) custom-call(bf16[2,4,64,512]{3,2,1,0:T(8,128)(2,1)} %copy-done.11, bf16[2,4,64,512]{3,2,1,0:T(8,128)(2,1)} %collective-permute-done.6.refs_1_, bf16[2,4,64,512]{3,2,1,0:T(8,128)(2,1)} %copy-done.25, ...), custom_call_target="tpu_custom_call" | custom-call | flops 8800000000 | bytes 28800000 | tf_op jit(solution)/shard_map/pallas_call | solution.py:963
  120.1 10.8 %shard_map.263 = (bf16[2,464,640]{2,1,0:T(8,128)(2,1)}, bf16[2,464,512]{2,1,0:T(8,128)(2,1)}, f32[2,128,512]{2,1,0:T(8,128)}, f32[2,128,512]{2,1,0:T(8,128)}) custom-call(bf16[2,4,64,512]{3,2,1,0:T(8,128)(2,1)} %copy-done.11, bf16[2,4,64,512]{3,2,1,0:T(8,128)(2,1)} %collective-permute-done.6.refs_1_, bf16[2,4,64,512]{3,2,1,0:T(8,128)(2,1)} %copy-done.25, ...), custom_call_target="tpu_custom_call" | custom-call | flops 8800000000 | bytes 28800000 | tf_op jit(solution)/shard_map/pallas_call | solution.py:963
  131.7 28.8 %shard_map.264 = (bf16[4,464,512]{2,1,0:T(8,128)(2,1)}, bf16[2,416,512]{2,1,0:T(8,128)(2,1)}, bf16[2,416,512]{2,1,0:T(8,128)(2,1)}, bf16[8,96,512]{2,1,0:T(8,128)(2,1)}) custom-call(bf16[2,4,64,512]{3,2,1,0:T(8,128)(2,1)} %copy-done.12, bf16[2,4,64,512]{3,2,1,0:T(8,128)(2,1)} %collective-permute-done.23.refs_1_, ...), custom_call_target="tpu_custom_call" | custom-call | flops 27499999232 | bytes 90000000 | tf_op jit(solution)/shard_map/pallas_call | solution.py:994
  160.6 2.6 %collective-permute-done.31.grad_b = bf16[2,416,512]{2,1,0:T(8,128)(2,1)S(1)} collective-permute-done((bf16[2,416,512]{2,1,0:T(8,128)(2,1)}, bf16[2,416,512]{2,1,0:T(8,128)(2,1)S(1)}, u32[]{:S(2)}, u32[]{:S(2)}) %collective-permute-start.31) | collective-permute-done | bytes 852000 | tf_op jit(solution)/shard_map/ppermute | solution.py:725
  165.1 6.0 %all-to-all-start.1 = ((bf16[8,96,512]{2,1,0:T(8,128)(2,1)}), bf16[8,96,512]{2,1,0:T(8,128)(2,1)S(1)}, u32[]{:S(2)}, u32[]{:S(2)}) async-start(bf16[8,96,512]{2,1,0:T(8,128)(2,1)} %get-tuple-element.138), calls=%async_computation.1 | async-start | bytes 1572864 | tf_op jit(solution)/shard_map/all_to_all | solution.py:1044
  171.1 7.5 %shard_map.265 = (bf16[2,416,512]{2,1,0:T(8,128)(2,1)}, bf16[2,416,512]{2,1,0:T(8,128)(2,1)}) custom-call(s32[16,128]{1,0:T(8,128)} %copy-done.9, f32[4,416,2]{2,1,0:T(8,128)} %bitcast.67, bf16[2,464,512]{2,1,0:T(8,128)(2,1)} %get-tuple-element.99.refs_0_, bf16[2,464,512]{2,1,0:T(8,128)(2,1)} %get-tuple-element.106.refs_1_, ...), custom_call_target="tpu_custom_call" | custom-call | flops 7699999744 | bytes 25200000 | tf_op jit(solution)/shard_map/pallas_call | solution.py:1031
  179.3 11.7 %shard_map.266 = (f32[416,512]{1,0:T(8,128)}, bf16[416,1536]{1,0:T(8,128)(2,1)}, bf16[416,384]{1,0:T(8,128)(2,1)}, bf16[32,32,128]{2,1,0:T(8,128)(2,1)}) custom-call(s32[8]{0:T(128)} %adapter.5, bf16[416,512]{1,0:T(8,128)(2,1)} %copy-done.2, f32[416,512]{1,0:T(8,128)} %get-tuple-element.129.middle, bf16[2,416,512]{2,1,0:T(8,128)(2,1)} %get-tuple-element.119.grad_a, ...), custom_call_target="tpu_custom_call" | custom-call | flops 12099999744 | bytes 39600000 | tf_op jit(solution)/shard_map/pallas_call | solution.py:90
  191.3 5.7 %all-to-all-start = ((bf16[32,32,128]{2,1,0:T(8,128)(2,1)}), bf16[32,32,128]{2,1,0:T(8,128)(2,1)S(1)}, u32[]{:S(2)}, u32[]{:S(2)}) async-start(bf16[32,32,128]{2,1,0:T(8,128)(2,1)} %get-tuple-element.128), calls=%async_computation | async-start | bytes 524288 | tf_op jit(solution)/shard_map/all_to_all | solution.py:1063
  197.8 1.7 collective-permute-done.35.rows_b
  199.6 1.8 collective-permute-start.36
  201.4 6.3 %all-to-all-done = bf16[32,32,128]{2,1,0:T(8,128)(2,1)S(1)} async-done(((bf16[32,32,128]{2,1,0:T(8,128)(2,1)}), bf16[32,32,128]{2,1,0:T(8,128)(2,1)S(1)}, u32[]{:S(2)}, u32[]{:S(2)}) %all-to-all-start) | async-done | bytes 262176 | tf_op jit(solution)/shard_map/all_to_all | solution.py:1063
  208.8 3.7 %all-to-all-start.2 = ((bf16[8,80,512]{2,1,0:T(8,128)(2,1)}), bf16[8,80,512]{2,1,0:T(8,128)(2,1)S(1)}, u32[]{:S(2)}, u32[]{:S(2)}) async-start(bf16[8,80,512]{2,1,0:T(8,128)(2,1)} %shard_map.270), calls=%async_computation.2 | async-start | bytes 1310720 | tf_op jit(solution)/shard_map/all_to_all | solution.py:1088
  213.0 5.5 %shard_map.268 = f32[394,512]{1,0:T(8,128)} custom-call(f32[416,512]{1,0:T(8,128)} %get-tuple-element.132.middle_grad, bf16[416,1536]{1,0:T(8,128)(2,1)} %get-tuple-element.133.proj_grad, bf16[416,384]{1,0:T(8,128)(2,1)} %get-tuple-element.134.code_grad, f32[416,512]{1,0:T(8,128)} %get-tuple-element.135.x_in, f32[2,512]{1,0:T(2,128)} %gain.5, ...), custom_call_target="tpu_custom_call" | custom-call | flops 5500000256 | bytes 18000000 | tf_op jit(solution)/shard_map/pallas_call | solution.py:1065
  218.5 5.8 %collective-permute-done.34.part_c = bf16[416,512]{1,0:T(8,128)(2,1)S(1)} collective-permute-done((bf16[416,512]{1,0:T(8,128)(2,1)S(1)}, bf16[416,512]{1,0:T(8,128)(2,1)S(1)}, u32[]{:S(2)}, u32[]{:S(2)}) %collective-permute-start.34) | collective-permute-done | bytes 426016 | tf_op jit(solution)/shard_map/ppermute | solution.py:725
  225.5 4.5 %all-to-all-done.2.came = bf16[8,80,512]{2,1,0:T(8,128)(2,1)S(1)} async-done(((bf16[8,80,512]{2,1,0:T(8,128)(2,1)}), bf16[8,80,512]{2,1,0:T(8,128)(2,1)S(1)}, u32[]{:S(2)}, u32[]{:S(2)}) %all-to-all-start.2) | async-done | bytes 655392 | tf_op jit(solution)/shard_map/all_to_all | solution.py:1088
  231.1 6.1 %collective-permute-done.38.side = bf16[256,512]{1,0:T(8,128)(2,1)S(1)} collective-permute-done((bf16[256,512]{1,0:T(8,128)(2,1)S(1)}, bf16[256,512]{1,0:T(8,128)(2,1)S(1)}, u32[]{:S(2)}, u32[]{:S(2)}) %collective-permute-start.38) | collective-permute-done | bytes 262176 | tf_op jit(solution)/shard_map/ppermute | solution.py:725
  (175 shorter events, 48.0 us)
Async XLA Ops:
  7.7 8.0 %collective-permute-start.2 = (bf16[2,272,128]{2,1,0:T(8,128)(2,1)S(1)}, bf16[2,272,128]{2,1,0:T(8,128)(2,1)S(1)}, u32[]{:S(2)}, u32[]{:S(2)}) collective-permute-start(bf16[2,272,128]{2,1,0:T(8,128)(2,1)S(1)} %pad_maximum_fusion.4.refs_0_), channel_id=1, source_target_pairs={{0,8},{4,12},{8,16},{12,20},{16,24},{20,28},{24,0},{28,4},{1,9},{5... | collective-permute-start | bytes 417800 | tf_op jit(solution)/shard_map/ppermute | solution.py:773
  12.7 16.8 %collective-permute-start.5 = (bf16[2,4,64,512]{3,2,1,0:T(8,128)(2,1)S(1)}, bf16[2,4,64,512]{3,2,1,0:T(8,128)(2,1)S(1)}, u32[]{:S(2)}, u32[]{:S(2)}) collective-permute-start(bf16[2,4,64,512]{3,2,1,0:T(8,128)(2,1)S(1)} %pad_maximum_fusion.1.refs_0_), channel_id=1, source_target_pairs={{0,8},{4,12},{8,16},{12,20},{16,24},{20,28},{24,0},{28,4},{1,9},{5... | collective-permute-start | bytes 1572872 | tf_op jit(solution)/shard_map/ppermute | solution.py:773
  14.3 15.2 %collective-permute-start.6 = (bf16[2,4,64,512]{3,2,1,0:T(8,128)(2,1)S(1)}, bf16[2,4,64,512]{3,2,1,0:T(8,128)(2,1)}, u32[]{:S(2)}, u32[]{:S(2)}) collective-permute-start(bf16[2,4,64,512]{3,2,1,0:T(8,128)(2,1)S(1)} %pad_maximum_fusion.1.refs_0_), channel_id=1, source_target_pairs={{0,4},{4,0},{8,12},{12,8},{16,20},{20,16},{24,28},{28,24},{1,5},{5... | collective-permute-start | bytes 1572872 | tf_op jit(solution)/shard_map/ppermute | solution.py:776
  15.7 13.8 %collective-permute-start.4 = (bf16[2,272,128]{2,1,0:T(8,128)(2,1)S(1)}, bf16[2,272,128]{2,1,0:T(8,128)(2,1)S(1)}, u32[]{:S(2)}, u32[]{:S(2)}) collective-permute-start(bf16[2,272,128]{2,1,0:T(8,128)(2,1)S(1)} %collective-permute-done.2.refs_2_), channel_id=1, source_target_pairs={{0,8},{4,12},{8,16},{12,20},{16,24},{20,28},{24,0},{28,4},{1,9},{5... | collective-permute-start | bytes 417800 | tf_op jit(solution)/shard_map/ppermute | solution.py:773
  17.4 11.8 %collective-permute-start.3 = (bf16[2,272,128]{2,1,0:T(8,128)(2,1)S(1)}, bf16[2,272,128]{2,1,0:T(8,128)(2,1)S(1)}, u32[]{:S(2)}, u32[]{:S(2)}) collective-permute-start(bf16[2,272,128]{2,1,0:T(8,128)(2,1)S(1)} %collective-permute-done.2.refs_2_), channel_id=1, source_target_pairs={{0,4},{4,0},{8,12},{12,8},{16,20},{20,16},{24,28},{28,24},{1,5},{5... | collective-permute-start | bytes 417800 | tf_op jit(solution)/shard_map/ppermute | solution.py:776
  23.3 16.8 %collective-permute-start.10 = (bf16[416,512]{1,0:T(8,128)(2,1)S(1)}, bf16[416,512]{1,0:T(8,128)(2,1)S(1)}, u32[]{:S(2)}, u32[]{:S(2)}) collective-permute-start(bf16[416,512]{1,0:T(8,128)(2,1)S(1)} %get-tuple-element.118.dy), channel_id=1, source_target_pairs={{0,2},{1,3},{2,0},{3,1},{4,6},{5,7},{6,4},{7,5},{8,10},{9,11},{10,... | collective-permute-start | bytes 1277960 | tf_op jit(solution)/shard_map/ppermute | solution.py:725
  43.7 17.8 %collective-permute-start.14 = (bf16[2,4,64,512]{3,2,1,0:T(8,128)(2,1)S(1)}, bf16[2,4,64,512]{3,2,1,0:T(8,128)(2,1)}, u32[]{:S(2)}, u32[]{:S(2)}) collective-permute-start(bf16[2,4,64,512]{3,2,1,0:T(8,128)(2,1)S(1)} %collective-permute-done.5.refs_2_), channel_id=1, source_target_pairs={{0,8},{4,12},{8,16},{12,20},{16,24},{20,28},{24,0},{28,4},{1,9},{5... | collective-permute-start | bytes 1572872 | tf_op jit(solution)/shard_map/ppermute | solution.py:773
  43.8 16.8 %collective-permute-start.13 = (bf16[2,4,64,512]{3,2,1,0:T(8,128)(2,1)S(1)}, bf16[2,4,64,512]{3,2,1,0:T(8,128)(2,1)S(1)}, u32[]{:S(2)}, u32[]{:S(2)}) collective-permute-start(bf16[2,4,64,512]{3,2,1,0:T(8,128)(2,1)S(1)} %collective-permute-done.5.refs_2_), channel_id=1, source_target_pairs={{0,4},{4,0},{8,12},{12,8},{16,20},{20,16},{24,28},{28,24},{1,5},{5... | collective-permute-start | bytes 1572872 | tf_op jit(solution)/shard_map/ppermute | solution.py:776
  57.4 12.2 %collective-permute-start.18 = (bf16[416,512]{1,0:T(8,128)(2,1)}, bf16[416,512]{1,0:T(8,128)(2,1)}, u32[]{:S(2)}, u32[]{:S(2)}) collective-permute-start(bf16[416,512]{1,0:T(8,128)(2,1)} %get-tuple-element.93.own), channel_id=1, source_target_pairs={{0,2},{1,3},{2,0},{3,1},{4,6},{5,7},{6,4},{7,5},{8,10},{9,11},{10,... | collective-permute-start | bytes 1277960 | tf_op jit(solution)/shard_map/ppermute | solution.py:725
  59.0 18.2 %collective-permute-start.20 = (bf16[2,416,512]{2,1,0:T(8,128)(2,1)S(1)}, bf16[2,416,512]{2,1,0:T(8,128)(2,1)}, u32[]{:S(2)}, u32[]{:S(2)}) collective-permute-start(bf16[2,416,512]{2,1,0:T(8,128)(2,1)S(1)} %pad_maximum_fusion.dy_near), channel_id=1, source_target_pairs={{0,1},{1,0},{2,3},{3,2},{4,5},{5,4},{6,7},{7,6},{8,9},{9,8},{10,11... | collective-permute-start | bytes 2555912 | tf_op jit(solution)/shard_map/ppermute | solution.py:725
  59.2 14.5 %collective-permute-start.23 = (bf16[2,4,64,512]{3,2,1,0:T(8,128)(2,1)S(1)}, bf16[2,4,64,512]{3,2,1,0:T(8,128)(2,1)}, u32[]{:S(2)}, u32[]{:S(2)}) collective-permute-start(bf16[2,4,64,512]{3,2,1,0:T(8,128)(2,1)S(1)} %pad_maximum_fusion.2.refs_0_), channel_id=1, source_target_pairs={{0,4},{4,0},{8,12},{12,8},{16,20},{20,16},{24,28},{28,24},{1,5},{5... | collective-permute-start | bytes 1572872 | tf_op jit(solution)/shard_map/ppermute | solution.py:776
  60.6 15.9 %collective-permute-start.22 = (bf16[2,4,64,512]{3,2,1,0:T(8,128)(2,1)S(1)}, bf16[2,4,64,512]{3,2,1,0:T(8,128)(2,1)}, u32[]{:S(2)}, u32[]{:S(2)}) collective-permute-start(bf16[2,4,64,512]{3,2,1,0:T(8,128)(2,1)S(1)} %pad_maximum_fusion.2.refs_0_), channel_id=1, source_target_pairs={{0,8},{4,12},{8,16},{12,20},{16,24},{20,28},{24,0},{28,4},{1,9},{5... | collective-permute-start | bytes 1572872 | tf_op jit(solution)/shard_map/ppermute | solution.py:773
  61.5 15.7 %collective-permute-start.17 = (bf16[416,512]{1,0:T(8,128)(2,1)}, bf16[416,512]{1,0:T(8,128)(2,1)S(1)}, u32[]{:S(2)}, u32[]{:S(2)}) collective-permute-start(bf16[416,512]{1,0:T(8,128)(2,1)} %get-tuple-element.93.own), channel_id=1, source_target_pairs={{0,1},{1,0},{2,3},{3,2},{4,5},{5,4},{6,7},{7,6},{8,9},{9,8},{10,11... | collective-permute-start | bytes 1277960 | tf_op jit(solution)/shard_map/ppermute | solution.py:725
  69.6 9.1 %collective-permute-start.19 = (bf16[416,512]{1,0:T(8,128)(2,1)}, bf16[416,512]{1,0:T(8,128)(2,1)S(1)}, u32[]{:S(2)}, u32[]{:S(2)}) collective-permute-start(bf16[416,512]{1,0:T(8,128)(2,1)} %collective-permute-done.18.side), channel_id=1, source_target_pairs={{0,1},{1,0},{2,3},{3,2},{4,5},{5,4},{6,7},{7,6},{8,9},{9,8},{10,11... | collective-permute-start | bytes 1277960 | tf_op jit(solution)/shard_map/ppermute | solution.py:725
  73.7 22.8 %collective-permute-start.16 = (bf16[2,4,64,512]{3,2,1,0:T(8,128)(2,1)}, bf16[2,4,64,512]{3,2,1,0:T(8,128)(2,1)S(1)}, u32[]{:S(2)}, u32[]{:S(2)}) collective-permute-start(bf16[2,4,64,512]{3,2,1,0:T(8,128)(2,1)} %collective-permute-done.14.refs_4_), channel_id=1, source_target_pairs={{0,8},{4,12},{8,16},{12,20},{16,24},{20,28},{24,0},{28,4},{1,9},{5... | collective-permute-start | bytes 1572872 | tf_op jit(solution)/shard_map/ppermute | solution.py:773
  76.5 19.4 %collective-permute-start.15 = (bf16[2,4,64,512]{3,2,1,0:T(8,128)(2,1)}, bf16[2,4,64,512]{3,2,1,0:T(8,128)(2,1)S(1)}, u32[]{:S(2)}, u32[]{:S(2)}) collective-permute-start(bf16[2,4,64,512]{3,2,1,0:T(8,128)(2,1)} %collective-permute-done.14.refs_4_), channel_id=1, source_target_pairs={{0,4},{4,0},{8,12},{12,8},{16,20},{20,16},{24,28},{28,24},{1,5},{5... | collective-permute-start | bytes 1572872 | tf_op jit(solution)/shard_map/ppermute | solution.py:776
  77.2 24.4 %collective-permute-start.24 = (bf16[2,4,64,512]{3,2,1,0:T(8,128)(2,1)}, bf16[2,4,64,512]{3,2,1,0:T(8,128)(2,1)S(1)}, u32[]{:S(2)}, u32[]{:S(2)}) collective-permute-start(bf16[2,4,64,512]{3,2,1,0:T(8,128)(2,1)} %collective-permute-done.22.refs_2_), channel_id=1, source_target_pairs={{0,8},{4,12},{8,16},{12,20},{16,24},{20,28},{24,0},{28,4},{1,9},{5... | collective-permute-start | bytes 1572872 | tf_op jit(solution)/shard_map/ppermute | solution.py:773
  77.2 25.7 %collective-permute-start.25 = (bf16[2,4,64,512]{3,2,1,0:T(8,128)(2,1)}, bf16[2,4,64,512]{3,2,1,0:T(8,128)(2,1)}, u32[]{:S(2)}, u32[]{:S(2)}) collective-permute-start(bf16[2,4,64,512]{3,2,1,0:T(8,128)(2,1)} %collective-permute-done.22.refs_2_), channel_id=1, source_target_pairs={{0,4},{4,0},{8,12},{12,8},{16,20},{20,16},{24,28},{28,24},{1,5},{5... | collective-permute-start | bytes 1572872 | tf_op jit(solution)/shard_map/ppermute | solution.py:776
  96.0 11.2 %collective-permute-start.26 = (bf16[2,2,64,512]{3,2,1,0:T(8,128)(2,1)S(1)}, bf16[2,2,64,512]{3,2,1,0:T(8,128)(2,1)S(1)}, u32[]{:S(2)}, u32[]{:S(2)}) collective-permute-start(bf16[2,2,64,512]{3,2,1,0:T(8,128)(2,1)S(1)} %slice.53), channel_id=1, source_target_pairs={{0,8},{4,12},{8,16},{12,20},{16,24},{20,28},{24,0},{28,4},{1,9},{5... | collective-permute-start | bytes 786440 | tf_op jit(solution)/shard_map/ppermute | solution.py:773
  96.5 10.7 %collective-permute-start.21 = (bf16[2,2,64,512]{3,2,1,0:T(8,128)(2,1)S(1)}, bf16[2,2,64,512]{3,2,1,0:T(8,128)(2,1)}, u32[]{:S(2)}, u32[]{:S(2)}) collective-permute-start(bf16[2,2,64,512]{3,2,1,0:T(8,128)(2,1)S(1)} %slice.50), channel_id=1, source_target_pairs={{0,4},{4,0},{8,12},{12,8},{16,20},{20,16},{24,28},{28,24},{1,5},{5... | collective-permute-start | bytes 786440 | tf_op jit(solution)/shard_map/ppermute | solution.py:776
  102.9 16.2 %collective-permute-start.27 = (bf16[2,4,64,512]{3,2,1,0:T(8,128)(2,1)S(1)}, bf16[2,4,64,512]{3,2,1,0:T(8,128)(2,1)S(1)}, u32[]{:S(2)}, u32[]{:S(2)}) collective-permute-start(bf16[2,4,64,512]{3,2,1,0:T(8,128)(2,1)S(1)} %collective-permute-done.24.refs_4_), channel_id=1, source_target_pairs={{0,8},{4,12},{8,16},{12,20},{16,24},{20,28},{24,0},{28,4},{1,9},{5... | collective-permute-start | bytes 1572872 | tf_op jit(solution)/shard_map/ppermute | solution.py:773
  107.2 12.6 %collective-permute-start.28 = (bf16[2,4,64,512]{3,2,1,0:T(8,128)(2,1)S(1)}, bf16[2,4,64,512]{3,2,1,0:T(8,128)(2,1)S(1)}, u32[]{:S(2)}, u32[]{:S(2)}) collective-permute-start(bf16[2,4,64,512]{3,2,1,0:T(8,128)(2,1)S(1)} %collective-permute-done.24.refs_4_), channel_id=1, source_target_pairs={{0,4},{4,0},{8,12},{12,8},{16,20},{20,16},{24,28},{28,24},{1,5},{5... | collective-permute-start | bytes 1572872 | tf_op jit(solution)/shard_map/ppermute | solution.py:776
  119.2 11.7 %collective-permute-start.29 = (bf16[2,2,64,512]{3,2,1,0:T(8,128)(2,1)S(1)}, bf16[2,2,64,512]{3,2,1,0:T(8,128)(2,1)S(1)}, u32[]{:S(2)}, u32[]{:S(2)}) collective-permute-start(bf16[2,2,64,512]{3,2,1,0:T(8,128)(2,1)S(1)} %slice.54), channel_id=1, source_target_pairs={{0,4},{4,0},{8,12},{12,8},{16,20},{20,16},{24,28},{28,24},{1,5},{5... | collective-permute-start | bytes 786440 | tf_op jit(solution)/shard_map/ppermute | solution.py:776
  119.8 11.1 %collective-permute-start.30 = (bf16[2,2,64,512]{3,2,1,0:T(8,128)(2,1)S(1)}, bf16[2,2,64,512]{3,2,1,0:T(8,128)(2,1)S(1)}, u32[]{:S(2)}, u32[]{:S(2)}) collective-permute-start(bf16[2,2,64,512]{3,2,1,0:T(8,128)(2,1)S(1)} %slice.55), channel_id=1, source_target_pairs={{0,8},{4,12},{8,16},{12,20},{16,24},{20,28},{24,0},{28,4},{1,9},{5... | collective-permute-start | bytes 786440 | tf_op jit(solution)/shard_map/ppermute | solution.py:773
  164.6 14.0 %collective-permute-start.32 = (bf16[416,512]{1,0:T(8,128)(2,1)S(1)}, bf16[416,512]{1,0:T(8,128)(2,1)S(1)}, u32[]{:S(2)}, u32[]{:S(2)}) collective-permute-start(bf16[416,512]{1,0:T(8,128)(2,1)S(1)} %fusion), channel_id=1, source_target_pairs={{0,2},{1,3},{2,0},{3,1},{4,6},{5,7},{6,4},{7,5},{8,10},{9,11},{10,... | collective-permute-start | bytes 1277960 | tf_op jit(solution)/shard_map/ppermute | solution.py:725
  165.1 26.2 %all-to-all-start.1 = ((bf16[8,96,512]{2,1,0:T(8,128)(2,1)}), bf16[8,96,512]{2,1,0:T(8,128)(2,1)S(1)}, u32[]{:S(2)}, u32[]{:S(2)}) async-start(bf16[8,96,512]{2,1,0:T(8,128)(2,1)} %get-tuple-element.138), calls=%async_computation.1 | async-start | bytes 1572864 | tf_op jit(solution)/shard_map/all_to_all | solution.py:1044
  191.3 16.3 %all-to-all-start = ((bf16[32,32,128]{2,1,0:T(8,128)(2,1)}), bf16[32,32,128]{2,1,0:T(8,128)(2,1)S(1)}, u32[]{:S(2)}, u32[]{:S(2)}) async-start(bf16[32,32,128]{2,1,0:T(8,128)(2,1)} %get-tuple-element.128), calls=%async_computation | async-start | bytes 524288 | tf_op jit(solution)/shard_map/all_to_all | solution.py:1063
  197.1 15.4 %collective-permute-start.33 = (bf16[2,416,512]{2,1,0:T(8,128)(2,1)S(1)}, bf16[2,416,512]{2,1,0:T(8,128)(2,1)S(1)}, u32[]{:S(2)}, u32[]{:S(2)}) collective-permute-start(bf16[2,416,512]{2,1,0:T(8,128)(2,1)S(1)} %copy-done.24), channel_id=1, source_target_pairs={{0,1},{1,0},{2,3},{3,2},{4,5},{5,4},{6,7},{7,6},{8,9},{9,8},{10,11... | collective-permute-start | bytes 2555912 | tf_op jit(solution)/shard_map/ppermute | solution.py:725
  199.6 8.1 %collective-permute-start.36 = (bf16[16,512]{1,0:T(8,128)(2,1)S(1)}, bf16[16,512]{1,0:T(8,128)(2,1)S(1)}, u32[]{:S(2)}, u32[]{:S(2)}) collective-permute-start(bf16[16,512]{1,0:T(8,128)(2,1)S(1)} %fusion.2), channel_id=1, source_target_pairs={{0,2},{1,3},{2,0},{3,1},{4,6},{5,7},{6,4},{7,5},{8,10},{9,11},{10,... | collective-permute-start | bytes 49160 | tf_op jit(solution)/shard_map/ppermute | solution.py:725
  208.8 21.3 %all-to-all-start.2 = ((bf16[8,80,512]{2,1,0:T(8,128)(2,1)}), bf16[8,80,512]{2,1,0:T(8,128)(2,1)S(1)}, u32[]{:S(2)}, u32[]{:S(2)}) async-start(bf16[8,80,512]{2,1,0:T(8,128)(2,1)} %shard_map.270), calls=%async_computation.2 | async-start | bytes 1310720 | tf_op jit(solution)/shard_map/all_to_all | solution.py:1088
  212.6 11.7 %collective-permute-start.34 = (bf16[416,512]{1,0:T(8,128)(2,1)S(1)}, bf16[416,512]{1,0:T(8,128)(2,1)S(1)}, u32[]{:S(2)}, u32[]{:S(2)}) collective-permute-start(bf16[416,512]{1,0:T(8,128)(2,1)S(1)} %fusion.1), channel_id=1, source_target_pairs={{0,2},{1,3},{2,0},{3,1},{4,6},{5,7},{6,4},{7,5},{8,10},{9,11},{10,... | collective-permute-start | bytes 1277960 | tf_op jit(solution)/shard_map/ppermute | solution.py:725
  230.1 7.1 %collective-permute-start.38 = (bf16[256,512]{1,0:T(8,128)(2,1)S(1)}, bf16[256,512]{1,0:T(8,128)(2,1)S(1)}, u32[]{:S(2)}, u32[]{:S(2)}) collective-permute-start(bf16[256,512]{1,0:T(8,128)(2,1)S(1)} %pad_maximum_fusion.3.own), channel_id=1, source_target_pairs={{0,2},{1,3},{2,0},{3,1},{4,6},{5,7},{6,4},{7,5},{8,10},{9,11},{10,... | collective-permute-start | bytes 786440 | tf_op jit(solution)/shard_map/ppermute | solution.py:725
  (45 other events, 438.2 us)
